TPU v7x, 32 devices: a whole 2x2x4 slice. The times are simulated.
32 devices in a mesh: rows: 4 (over x, core), cols: 8 (over z, y).
Axes of the slice: x: 2, y: 2, z: 4, core: 2. Of those that a mesh axis runs over, the one named last changes fastest.
Arguments:
- blocks: bfloat16 [48, 48, 256, 256], P('rows', 'cols'), may hold values from -1.5 to 1.5
- pattern: int32 [48, 48], P('rows', 'cols'), may hold values 0 or 1
- pivot_inverse: bfloat16 [2, 256, 256], replicated, may hold values from -0.375 to 0.375
- right_sides: float32 [48, 3, 256], P('rows'), may hold values from -6 to 6
Outputs:
- factored: bfloat16 [48, 48, 256, 256], P('rows', 'cols')
- forward: float32 [48, 3, 256], P('rows')
All inputs are finite; a program needn't handle non-finite values. No bound on the sum of `pattern` on one device may be relied on, other than what follows from the above.
Results may differ from a plain program's by a relative error of at most 0.0071.
Values may be sent and summed in bfloat16 or wider, within the bound.
No kernel may reach another device: no remote copies, remote signals or barrier semaphores. Data moves between devices by JAX's collectives and lax.ppermute only.
A program may use at most 128 MiB of HBM per device.

v0:
```python
import jax
import jax.numpy as jnp
from jax import lax
from jax.sharding import PartitionSpec as P


def spread(x, axis, root):
    mine = lax.axis_index(axis) == root
    return lax.psum(jnp.where(mine, x, jnp.zeros_like(x)), axis)


def schur(part, lower, upper, live_part):
    prod = jnp.einsum("iab,jbc->ijac", lower, upper, preferred_element_type=jnp.float32)
    fresh = (part.astype(jnp.float32) - prod).astype(jnp.bfloat16)
    return jnp.where(live_part[:, :, None, None], fresh, part)


def on_device(blocks, pattern, pivot_inverse, right_sides):
    row_count = blocks.shape[0]
    nrows = lax.axis_size("rows")
    ncols = lax.axis_size("cols")
    row_glob = jnp.arange(row_count) * nrows + lax.axis_index("rows")
    col_glob = jnp.arange(blocks.shape[1]) * ncols + lax.axis_index("cols")
    live = pattern == 1
    zero_block = jnp.zeros((), jnp.bfloat16)
    matrix = jnp.where(live[:, :, None, None], blocks, zero_block)

    def column_panel(column, step):
        scaled = jnp.einsum(
            "nab,bc->nac", column, pivot_inverse[step], preferred_element_type=jnp.float32
        ).astype(jnp.bfloat16)
        landed = spread(scaled, "cols", step % ncols)
        return jnp.where((row_glob > step)[:, None, None], landed, zero_block)

    def pivot_panel(rowblocks, step):
        landed = spread(rowblocks, "rows", step % nrows)
        return jnp.where((col_glob > step)[:, None, None], landed, zero_block)

    def place_lower(matrix, lower, step):
        where_lower = (col_glob == step)[None, :] & (row_glob > step)[:, None]
        return jnp.where(where_lower[:, :, None, None], lower[:, None], matrix)

    lower_zero = column_panel(matrix[:, 0], 0)
    upper_zero = pivot_panel(matrix[0], 0)
    matrix = schur(matrix, lower_zero, upper_zero, live)
    lower_one = column_panel(matrix[:, 0], 1)
    upper_one = pivot_panel(matrix[0], 1)
    matrix = place_lower(matrix, lower_zero, 0)
    matrix = schur(matrix, lower_one, upper_one, live)
    matrix = place_lower(matrix, lower_one, 1)
    first = spread(right_sides[0], "rows", 0)
    rhs = right_sides - jnp.einsum(
        "nab,cb->nca", lower_zero.astype(jnp.float32), first, precision=lax.Precision.HIGHEST
    )
    second = spread(rhs[1 // nrows], "rows", 1 % nrows)
    rhs = rhs - jnp.einsum(
        "nab,cb->nca", lower_one.astype(jnp.float32), second, precision=lax.Precision.HIGHEST
    )
    return (matrix, rhs)


def solution(mesh):
    return jax.shard_map(
        on_device,
        mesh=mesh,
        in_specs=(P("rows", "cols", None, None), P("rows", "cols"), P(), P("rows", None, None)),
        out_specs=(P("rows", "cols", None, None), P("rows", None, None)),
        check_vma=False,
    )
```

profile of v0, /device:TPU:0, one launch (start us, length us, event | category | flops | bytes accessed | tf_op | source)
XLA Modules:
  0.0 309.3 jit_solution(4847109239567418238)
XLA Ops:
  7.2 0.7 broadcast_compare_fusion
  7.9 8.2 %copy_select_fusion = bf16[12,6,256,256]{3,2,0,1:T(8,128)(2,1)} fusion(bf16[12,6,256,256]{3,2,1,0:T(8,128)(2,1)} %param.4, pred[12,6]{0,1:T(8,128)(4,1)S(1)} %broadcast_compare_fusion), kind=kLoop, calls=%fused_computation.7 | loop fusion | flops 4718592 | bytes 18874440 | tf_op jit(solution)/shard_map/jit(_where)/select_n | solution.py:26
  16.1 3.1 %broadcast_select_fusion.2 = bf16[12,256,256]{2,1,0:T(8,128)(2,1)} fusion(pred[]{:T(512)S(6)} %eq.39, bf16[12,6,256,256]{3,2,0,1:T(8,128)(2,1)} %copy_select_fusion, bf16[2,256,256]{2,1,0:T(8,128)(2,1)S(1)} %copy-done.2), kind=kOutput, calls=%fused_computation.16 | convolution fusion | flops 404226048 | bytes 3276801 | tf_op jit(solution)/shard_map/nab,bc->nac/dot_general | solution.py:29
  19.2 0.0 all-reduce.5.cloned.1.call-start
  19.3 2.1 fusion.11
  21.4 0.0 all-reduce.9.cloned.1.call-start
  21.5 89.6 %all-reduce.7.cloned.1.call-done = bf16[12,256,256]{2,1,0:T(8,128)(2,1)} async-done(((bf16[12,256,256]{2,1,0:T(8,128)(2,1)}), bf16[12,256,256]{2,1,0:T(8,128)(2,1)}) %all-reduce.7.cloned.1.call-update) | async-done | bytes 1572880 | tf_op jit(solution)/shard_map/psum | solution.py:9
  111.1 1.6 broadcast_select_fusion
  112.7 34.8 %all-reduce.5.cloned.1.call-done = bf16[6,256,256]{2,1,0:T(8,128)(2,1)} async-done(((bf16[6,256,256]{2,1,0:T(8,128)(2,1)}), bf16[6,256,256]{2,1,0:T(8,128)(2,1)}) %all-reduce.5.cloned.1.call-update) | async-done | bytes 786448 | tf_op jit(solution)/shard_map/psum | solution.py:9
  147.5 6.5 %fusion.2 = bf16[12,6,256,256]{3,2,0,1:T(8,128)(2,1)S(1)} fusion(pred[12,6]{0,1:T(8,128)(4,1)S(1)} %broadcast_compare_fusion, bf16[12,256,256]{2,1,0:T(8,128)(2,1)S(1)} %broadcast_select_fusion, bf16[6,256,256]{2,1,0:T(8,128)(2,1)} %all-reduce.5.cloned.1.call-done, pred[6]{0:T(512)(128)(4,1)S(1)} %broadcast_compare_fusion.2, bf16[12,6,256,256]{3,2,1,0:T(8,128)(2,1)} %param.4), kind=kOutput, calls=%fused_computation.4 | convolution fusion | flops 2439905280 | bytes 21233742 | tf_op jit(solution)/shard_map/iab,jbc->ijac/dot_general | solution.py:13
  153.9 3.7 %copy-done = bf16[12,6,256,256]{3,2,0,1:T(8,128)(2,1)} copy-done((bf16[12,6,256,256]{3,2,0,1:T(8,128)(2,1)}, bf16[12,6,256,256]{3,2,0,1:T(8,128)(2,1)S(1)}, u32[]{:S(2)}) %copy-start) | copy-done | bytes 9437208
  157.7 1.7 broadcast_select_fusion.3
  159.5 5.8 %psum.46 = f32[3,256]{1,0:T(4,128)S(1)} all-reduce(f32[3,256]{1,0:T(4,128)S(1)} %select_bitcast_fusion), channel_id=1, replica_groups=mesh['rows'=4,'cols'=8] {'rows'}, use_global_device_ids=true, to_apply=%region_4.5 | all-reduce | flops 768 | bytes 6144 | tf_op jit(solution)/shard_map/psum | solution.py:9
  165.4 0.1 broadcast_and_fusion
  165.4 0.1 broadcast_and_fusion.1
  165.5 1.3 fusion.8
  166.8 6.1 %psum.47 = f32[3,256]{1,0:T(4,128)S(1)} all-reduce(f32[3,256]{1,0:T(4,128)S(1)} %fusion.24), channel_id=1, replica_groups=mesh['rows'=4,'cols'=8] {'rows'}, use_global_device_ids=true, to_apply=%region_5.6 | all-reduce | flops 768 | bytes 6144 | tf_op jit(solution)/shard_map/psum | solution.py:9
  172.9 2.1 fusion.9
  175.0 73.6 %all-reduce.9.cloned.1.call-done = bf16[12,256,256]{2,1,0:T(8,128)(2,1)} async-done(((bf16[12,256,256]{2,1,0:T(8,128)(2,1)}), bf16[12,256,256]{2,1,0:T(8,128)(2,1)}) %all-reduce.9.cloned.1.call-update) | async-done | bytes 1572880 | tf_op jit(solution)/shard_map/psum | solution.py:9
  248.6 1.6 broadcast_select_fusion.1
  250.2 2.0 fusion.7
  252.1 32.7 %all-reduce.11.cloned.1.call-done = bf16[6,256,256]{2,1,0:T(8,128)(2,1)} async-done(((bf16[6,256,256]{2,1,0:T(8,128)(2,1)}), bf16[6,256,256]{2,1,0:T(8,128)(2,1)}) %all-reduce.11.cloned.1.call-update) | async-done | bytes 786448 | tf_op jit(solution)/shard_map/psum | solution.py:9
  284.9 9.3 %fusion.4 = bf16[12,6,256,256]{3,2,0,1:T(8,128)(2,1)} fusion(bf16[12,6,256,256]{3,2,0,1:T(8,128)(2,1)} %copy-done, pred[12,6]{0,1:T(8,128)(4,1)S(1)} %broadcast_and_fusion, pred[12,6]{0,1:T(8,128)(4,1)S(1)} %broadcast_compare_fusion, pred[12,6]{0,1:T(8,128)(4,1)S(1)} %broadcast_and_fusion.1, bf16[12,256,256]{2,1,0:T(8,128)(2,1)S(1)} %broadcast_select_fusion, ...), kind=kOutput, calls=%fused_computation.6 | convolution fusion | flops 2444623872 | bytes 22806750 | tf_op jit(solution)/shard_map/iab,jbc->ijac/dot_general | solution.py:13
  294.2 8.6 %copy.13 = bf16[12,6,256,256]{3,2,1,0:T(8,128)(2,1)} copy(bf16[12,6,256,256]{3,2,0,1:T(8,128)(2,1)} %fusion.4) | data formatting | bytes 18874368
  (18 shorter events, 0.2 us)
Async XLA Ops:
  7.2 103.9 %all-reduce.7.cloned.1.call-start = ((), (), s32[]{:S(2)}) async-start(), calls=%async_computation.1 | async-start | bytes 3145728 | tf_op jit(solution)/shard_map/psum | solution.py:9
  7.9 8.2 %copy-start.2 = (bf16[2,256,256]{2,1,0:T(8,128)(2,1)S(1)}, bf16[2,256,256]{2,1,0:T(8,128)(2,1)}, u32[]{:S(2)}) copy-start(bf16[2,256,256]{2,1,0:T(8,128)(2,1)} %param.6) | copy-start | bytes 786436
  19.2 128.2 %all-reduce.5.cloned.1.call-start = ((), (), s32[]{:S(2)}) async-start(), calls=%async_computation | async-start | bytes 1572864 | tf_op jit(solution)/shard_map/psum | solution.py:9
  21.4 227.2 %all-reduce.9.cloned.1.call-start = ((), (), s32[]{:S(2)}) async-start(), calls=%async_computation.2 | async-start | bytes 3145728 | tf_op jit(solution)/shard_map/psum | solution.py:9
  153.9 3.7 %copy-start = (bf16[12,6,256,256]{3,2,0,1:T(8,128)(2,1)}, bf16[12,6,256,256]{3,2,0,1:T(8,128)(2,1)S(1)}, u32[]{:S(2)}) copy-start(bf16[12,6,256,256]{3,2,0,1:T(8,128)(2,1)S(1)} %fusion.2) | copy-start | bytes 28311556
  157.7 1.8 copy-start.1
  159.4 125.4 %all-reduce.11.cloned.1.call-start = ((), (), s32[]{:S(2)}) async-start(), calls=%async_computation.3 | async-start | bytes 1572864 | tf_op jit(solution)/shard_map/psum | solution.py:9
Sparse Core Ops, SparseCore 0:
  19.4 91.6 all-reduce.6
  113.4 33.9 all-reduce.4
  159.5 89.0 all-reduce.8
  250.8 33.9 all-reduce.10
where the time goes:
time: 310 us; the launch traced here: 309 us
  waiting for transfers between devices  231 us (75%)
  matrix products  23.9 us (8%)
  other arithmetic  16.4 us (5%)
  between operations  13.9 us (4%)
  local copies, waits for them, and re-layouts  12.3 us (4%)
  blocking collectives  11.9 us (4%)
    psum x4, waiting for transfers between devices, spread(): return lax.psum(jnp.where(mine, x, jnp.zeros_like(x)), axis)  231 us
    dot_general x2, matrix products, schur(): jnp.einsum('iab,jbc->ijac', lower, upper, preferred_element_type=jnp.floa...  15.8 us
    unnamed x7, local copies, waits for them, and re-layouts  12.3 us
    psum x2, blocking collectives, spread(): return lax.psum(jnp.where(mine, x, jnp.zeros_like(x)), axis)  11.9 us
    select_n x1, other arithmetic, on_device(): matrix = jnp.where(live[:, :, None, None], blocks, zero_block)  8.17 us
  transfers between devices with their start and end apart: 4, of which 4 were waited for; matrix products, arithmetic and copies ran while one was open for 3% of the time, Pallas kernels for 0%

commit v1 on v0

v1 whole, which is shorter than its diff:
```python
import functools

import jax
import jax.numpy as jnp
from jax import lax
from jax.experimental import pallas as pl
from jax.experimental.pallas import tpu as pltpu
from jax.sharding import PartitionSpec as P

BF = jnp.bfloat16
F32 = jnp.float32
FLAG_ROWS = 16
PIECE_ROWS = 32
MOST_CHUNKS = 4
VMEM_LIMIT = 40 * 1024 * 1024


def broadcast_plan(groups):
    children = {g: [] for g in range(groups)}

    def hang(low, high, parent):
        if low < high:
            hub = (low + high) // 2
            children[parent].append(hub)
            hang(low, hub, hub)
            hang(hub + 1, high, hub)

    hang(1, groups, 0)
    depth = {0: 0}
    order = [0]
    for g in order:
        for child in children[g]:
            depth[child] = depth[g] + 1
            order.append(child)
    edges = [(g, child, 0) for g in order for child in children[g]]
    spare = {g: 2 - len(children[g]) for g in order}
    orphans = []
    for g in order:
        if spare[g]:
            edges.append((g, g, 1))
            spare[g] -= 1
        else:
            orphans.append(g)
    for g in orphans:
        helper = min((h for h in order if spare[h]), key=lambda h: (depth[h], -h))
        edges.append((helper, g, 1))
        spare[helper] -= 1
    colour = {}
    for start in range(len(edges)):
        if start in colour:
            continue
        colour[start] = 0
        stack = [start]
        while stack:
            e = stack.pop()
            for f in range(len(edges)):
                if f != e and f not in colour and (edges[f][0] == edges[e][0] or edges[f][1] == edges[e][1]):
                    colour[f] = 1 - colour[e]
                    stack.append(f)
    permutes = ([], [])
    own_from, other_from, other_depth = {0: 0}, {}, {}
    for e, (sender, receiver, cross) in enumerate(edges):
        for side in (0, 1):
            permutes[colour[e]].append((2 * sender + side, 2 * receiver + (side ^ cross)))
        if cross:
            other_from[receiver] = colour[e]
            other_depth[receiver] = depth[sender]
        else:
            own_from[receiver] = colour[e]
    return depth, own_from, other_depth, other_from, permutes


def dot(a, b):
    return jnp.dot(a, b, preferred_element_type=F32)


def dot_t(a, b):
    return lax.dot_general(a, b, (((1,), (1,)), ((), ())), preferred_element_type=F32)


def pieces_of(rows):
    n, w = rows.shape
    full = jnp.concatenate([rows, jnp.zeros((8 - n, w), F32)], 0) if n < 8 else rows
    high = full.astype(BF).astype(F32)
    middle = (full - high).astype(BF).astype(F32)
    low = full - high - middle
    return jnp.concatenate([high, middle, low, jnp.zeros((PIECE_ROWS - 24, w), F32)], 0).astype(BF)


def sum_pieces(x, n):
    return (x[0:8] + x[8:16] + x[16:24])[:n]


def prepare_kernel(chunk, pattern, column, row, rhs, column_out, row_out):
    rows, width = column.shape[0], column.shape[-1]
    cols = row.shape[1]
    lines = lax.broadcasted_iota(jnp.int32, (FLAG_ROWS, width), 0)
    for k in range(rows // chunk):
        flags = jnp.zeros((FLAG_ROWS, width), F32)
        for i in range(chunk):
            live = pattern[k * chunk + i, 0] == 1
            column_out[k, i * width : (i + 1) * width] = jnp.where(live, column[k * chunk + i, 0], jnp.zeros((), BF))
            flags = jnp.where((lines == i) & live, 1.0, flags)
        column_out[k, chunk * width : chunk * width + FLAG_ROWS] = flags.astype(BF)
    flags = jnp.zeros((FLAG_ROWS, width), F32)
    for j in range(cols):
        live = pattern[0, j] == 1
        row_out[j * width : (j + 1) * width] = jnp.where(live, row[0, j], jnp.zeros((), BF))
        flags = jnp.where((lines == j) & live, 1.0, flags)
    base = cols * width
    row_out[base : base + FLAG_ROWS] = flags.astype(BF)
    row_out[base + FLAG_ROWS : base + FLAG_ROWS + PIECE_ROWS] = pieces_of(rhs[0])


def prepare(blocks, pattern, right_sides, chunk):
    rows, cols, width, _ = blocks.shape
    dirs = right_sides.shape[1]
    n = rows // chunk
    return pl.pallas_call(
        functools.partial(prepare_kernel, chunk),
        grid=(1,),
        in_specs=[
            pl.BlockSpec(memory_space=pltpu.SMEM),
            pl.BlockSpec((rows, 1, width, width), lambda s: (0, 0, 0, 0)),
            pl.BlockSpec((1, cols, width, width), lambda s: (0, 0, 0, 0)),
            pl.BlockSpec((1, dirs, width), lambda s: (0, 0, 0)),
        ],
        out_specs=[
            pl.BlockSpec((n, chunk * width + FLAG_ROWS, width), lambda s: (0, 0, 0)),
            pl.BlockSpec((cols * width + FLAG_ROWS + PIECE_ROWS, width), lambda s: (0, 0)),
        ],
        out_shape=[
            jax.ShapeDtypeStruct((n, chunk * width + FLAG_ROWS, width), BF),
            jax.ShapeDtypeStruct((cols * width + FLAG_ROWS + PIECE_ROWS, width), BF),
        ],
        compiler_params=pltpu.CompilerParams(vmem_limit_bytes=VMEM_LIMIT),
    )(pattern, blocks, blocks, right_sides)


def panel_kernel(dirs, ncols, mine, other, corner, other_corner, inverse, upper, upper_one, sides):
    width = inverse.shape[-1]
    cols = upper.shape[0]
    even = lax.axis_index("rows") % 2 == 0
    col = lax.axis_index("cols")

    def pick(lo, hi):
        a, b = mine[lo:hi], other[lo:hi]
        return jnp.where(even, a, b), jnp.where(even, b, a)

    zero = jnp.zeros((), BF)
    upper_one[...] = jnp.where(even, corner[...], other_corner[...])
    lower_one = dot(jnp.where(even, other_corner[...], corner[...]), inverse[0]).astype(BF)
    base = cols * width
    flags = pick(base, base + FLAG_ROWS)[1].astype(F32)
    for j in range(cols):
        zeroth, first = pick(j * width, (j + 1) * width)
        zeroth = jnp.where(j * ncols + col > 0, zeroth, zero)
        fresh = (first.astype(F32) - dot(lower_one, zeroth)).astype(BF)
        keep = (flags[j : j + 1] > 0.5) & (j * ncols + col > 1)
        upper[j, 0:width] = zeroth
        upper[j, width : 2 * width] = jnp.where(keep, fresh, zero)
    side_zero, side_one = pick(base + FLAG_ROWS, base + FLAG_ROWS + PIECE_ROWS)
    sides[0] = side_zero
    later = sum_pieces(side_one.astype(F32), dirs) - sum_pieces(dot_t(side_zero, lower_one), dirs)
    sides[1] = pieces_of(later)


def panel(dirs, cols, ncols, mine, other, corner, other_corner, inverse):
    width = inverse.shape[-1]
    return pl.pallas_call(
        functools.partial(panel_kernel, dirs, ncols),
        out_shape=[
            jax.ShapeDtypeStruct((cols, 2 * width, width), BF),
            jax.ShapeDtypeStruct((width, width), BF),
            jax.ShapeDtypeStruct((2, PIECE_ROWS, width), BF),
        ],
        compiler_params=pltpu.CompilerParams(vmem_limit_bytes=VMEM_LIMIT),
        cost_estimate=pl.CostEstimate(
            flops=2 * (cols + 2) * width**3, bytes_accessed=8 * cols * width**2, transcendentals=0
        ),
    )(mine, other, corner, other_corner, inverse)


def update_kernel(chunk, index, nrows, ncols, sources, n_refs, aliased, *refs):
    pattern, blocks, rhs, upper, upper_one, sides, inverse = refs[:7]
    landed = refs[7 : 7 + n_refs]
    out, forward, columns, sems = refs[7 + n_refs + aliased :]
    width = inverse.shape[-1]
    cols = blocks.shape[1]
    row_device, col = lax.axis_index("rows"), lax.axis_index("cols")
    pair, side = col // 2, col % 2
    step = pl.program_id(0)

    @pl.when(step == 0)
    def _():
        for which in (0, 1):
            for ref, pairs in sources[which]:
                hit = functools.reduce(jnp.logical_or, [pair == g for g in pairs])
                source = landed[ref[0]] if ref[1] is None else landed[ref[0]].at[ref[1]]

                @pl.when(hit)
                def _(source=source, which=which):
                    place = side if which == 0 else 1 - side
                    pltpu.make_async_copy(source, columns.at[place], sems.at[which]).start()

        for which in (0, 1):
            pltpu.make_async_copy(columns.at[which], columns.at[which], sems.at[which]).wait()

    local = index * chunk + step
    here = local * nrows + row_device
    zero = jnp.zeros((), BF)
    at = pl.ds(pl.multiple_of(step * width, width), width)
    lower_zero = dot(columns[0, at], inverse[0]).astype(BF)
    lower_zero = jnp.where(here > 0, lower_zero, zero)
    flags = columns[1, chunk * width : chunk * width + FLAG_ROWS].astype(F32)
    lines = lax.broadcasted_iota(jnp.int32, flags.shape, 0)
    live = jnp.sum(jnp.where(lines == step, flags, 0.0), 0, keepdims=True) > 0.5
    pivot = (columns[1, at].astype(F32) - dot(lower_zero, upper_one[...])).astype(BF)
    lower_one = dot(jnp.where(live, pivot, zero), inverse[1]).astype(BF)
    lower_one = jnp.where(here > 1, lower_one, zero)
    lower = jnp.concatenate([lower_zero, lower_one], 1)
    for j in range(cols):
        keep = pattern[local, j] == 1

        @pl.when(keep)
        def _(j=j):
            out[0, j] = (blocks[0, j].astype(F32) - dot(lower, upper[j])).astype(BF)

        @pl.when(jnp.logical_not(keep))
        def _(j=j):
            out[0, j] = jnp.zeros((width, width), BF)

    @pl.when((col == 0) & (here > 0))
    def _():
        out[0, 0] = lower_zero

    @pl.when((col == 1) & (here > 1))
    def _():
        out[0, 0] = lower_one

    dirs = rhs.shape[1]
    first = rhs[0] - sum_pieces(dot_t(sides[0], lower_zero), dirs)
    forward[0] = first - sum_pieces(dot_t(sides[1], lower_one), dirs)


def update(chunk, index, nrows, ncols, sources, landed, pattern, blocks, rhs, upper, upper_one, sides, inverse, before):
    rows, cols, width, _ = blocks.shape
    dirs = rhs.shape[1]
    aliased = 0 if before is None else 2
    whole = pl.BlockSpec(memory_space=pltpu.VMEM)
    far = pl.BlockSpec(memory_space=pl.ANY)
    block_spec = pl.BlockSpec((1, cols, width, width), lambda s: (index * chunk + s, 0, 0, 0))
    rhs_spec = pl.BlockSpec((1, dirs, width), lambda s: (index * chunk + s, 0, 0))
    n_in = 7 + len(landed)
    return pl.pallas_call(
        functools.partial(update_kernel, chunk, index, nrows, ncols, sources, len(landed), aliased),
        grid=(chunk,),
        in_specs=[pl.BlockSpec(memory_space=pltpu.SMEM), block_spec, rhs_spec]
        + [whole] * 4
        + [far] * (len(landed) + aliased),
        out_specs=[block_spec, rhs_spec],
        out_shape=[jax.ShapeDtypeStruct(blocks.shape, BF), jax.ShapeDtypeStruct(rhs.shape, F32)],
        scratch_shapes=[
            pltpu.VMEM((2, chunk * width + FLAG_ROWS, width), BF),
            pltpu.SemaphoreType.DMA((2,)),
        ],
        input_output_aliases={n_in: 0, n_in + 1: 1} if aliased else {},
        compiler_params=pltpu.CompilerParams(vmem_limit_bytes=VMEM_LIMIT),
        cost_estimate=pl.CostEstimate(
            flops=4 * chunk * (cols + 2) * width**3, bytes_accessed=4 * chunk * (cols + 2) * width**2, transcendentals=0
        ),
    )(pattern, blocks, rhs, upper, upper_one, sides, inverse, *landed, *(before or ()))


def on_device(blocks, pattern, pivot_inverse, right_sides):
    rows, cols, width, _ = blocks.shape
    dirs = right_sides.shape[1]
    nrows = lax.axis_size("rows")
    ncols = lax.axis_size("cols")
    pair = lax.axis_index("cols") // 2
    side = lax.axis_index("cols") % 2
    row_device = lax.axis_index("rows")
    groups = ncols // 2
    depth, own_from, other_depth, other_from, permutes = broadcast_plan(groups)
    n = max(d for d in range(1, MOST_CHUNKS + 1) if rows % d == 0)
    chunk = rows // n
    columns, row = prepare(blocks, pattern, right_sides, chunk)

    def among(members):
        return functools.reduce(jnp.logical_or, [pair == g for g in members])

    def down_rows(x):
        reach = 1
        while reach < nrows // 2:
            hops = [(2 * h + s, 2 * (h + reach) + s) for h in range(min(reach, nrows // 2 - reach)) for s in (0, 1)]
            x = jnp.where(row_device < 2 * reach, x, lax.ppermute(x, "rows", hops))
            reach *= 2
        return x, lax.ppermute(x, "rows", [(r, r ^ 1) for r in range(nrows)])

    by_second = [g for g in range(1, groups) if own_from[g] == 1]
    deepest = max(other_depth.values())
    landed = []
    for step in range(n + deepest):
        payload = columns[step] if step < n else None
        if step:
            first, second = landed[step - 1]
            moved = jnp.where(among(by_second), second, first) if by_second else first
            payload = moved if payload is None else jnp.where(pair == 0, payload, moved)
        landed.append([lax.ppermute(payload, "cols", pairs) for pairs in permutes])

    mine, other = down_rows(row)

    def places(k):
        own, cross = {}, {}
        for g in range(groups):
            key = ("here",) if g == 0 else (own_from[g], k + depth[g] - 1)
            own.setdefault(key, []).append(g)
            cross.setdefault((other_from[g], k + other_depth[g]), []).append(g)
        return own, cross

    def array_at(key):
        return landed[key[1]][key[0]]

    own, cross = places(0)
    mine_first = columns[0, :width]
    for key, members in own.items():
        if key != ("here",):
            mine_first = jnp.where(among(members), array_at(key)[:width], mine_first)
    other_first = None
    for key, members in cross.items():
        piece = array_at(key)[:width]
        other_first = piece if other_first is None else jnp.where(among(members), piece, other_first)
    corner = jnp.where((side == 0) == (row_device == 1), mine_first, other_first)
    corner, other_corner = down_rows(corner)
    upper, upper_one, sides = panel(dirs, cols, ncols, mine, other, corner, other_corner, pivot_inverse)

    before = None
    for k in range(n):
        arrays, sources = [columns], []
        for which in places(k):
            found = []
            for key, members in which.items():
                if key == ("here",):
                    found.append(((0, k), members))
                else:
                    arrays.append(array_at(key))
                    found.append(((len(arrays) - 1, None), members))
            sources.append(found)
        before = update(
            chunk, k, nrows, ncols, sources, arrays, pattern, blocks, right_sides, upper, upper_one, sides,
            pivot_inverse, before,
        )
    return tuple(before)


def solution(mesh):
    return jax.shard_map(
        on_device,
        mesh=mesh,
        in_specs=(P("rows", "cols", None, None), P("rows", "cols"), P(), P("rows", None, None)),
        out_specs=(P("rows", "cols", None, None), P("rows", None, None)),
        check_vma=False,
    )
```

time: 310 us -> 107 us (0.35)
  waiting for transfers between devices: 231 us -> 26.9 us
  starting transfers between devices: 0.16 us -> 42.5 us
  Pallas kernels: 0 us -> 27.9 us
  matrix products: 23.9 us -> 0 us
  other arithmetic: 16.4 us -> 2.4 us
  between operations: 13.9 us -> 0.87 us
  blocking collectives: 11.9 us -> 0 us
  local copies, waits for them, and re-layouts: 12.3 us -> 5.31 us
    psum x4 -> x0, waiting for transfers between devices: 231 us -> none  [spread(): return lax.psum(jnp.where(mine, x, jnp.zeros_like(x)), axis)]
    ppermute x0 -> x16, starting transfers between devices: none -> 42.5 us  [the longest x12 34.9 us: on_device(): landed.append([lax.ppermute(payload, 'cols', pairs) for pairs in permutes])]
    pallas_call x0 -> x6, Pallas kernels: none -> 27.9 us  [the longest x4 25.8 us: update(): pl.pallas_call(functools.partial(update_kernel, chunk, index, nrows, ncol...]
    ppermute x0 -> x16, waiting for transfers between devices: none -> 26.9 us  [the longest x12 25.6 us: on_device(): landed.append([lax.ppermute(payload, 'cols', pairs) for pairs in permutes])]
    dot_general x6 -> x0, matrix products: 23.9 us -> none  [the longest x2 15.8 us: schur(): jnp.einsum('iab,jbc->ijac', lower, upper, preferred_element_type=jnp.floa...]
    select_n x7 -> x8, other arithmetic: 15.5 us -> 2.4 us  [the longest x2 1.25 us: down_rows(): x = jnp.where(row_device < 2 * reach, x, lax.ppermute(x, 'rows', hops))]
    psum x2 -> x0, blocking collectives: 11.9 us -> none  [spread(): return lax.psum(jnp.where(mine, x, jnp.zeros_like(x)), axis)]
    unnamed x7 -> x17, local copies, waits for them, and re-layouts: 12.3 us -> 5.28 us
  transfers between devices with their start and end apart: 4 -> 16, of which waited for: 4 -> 9; matrix products, arithmetic and copies ran while one was open for 3% -> 2% of each run, Pallas kernels for 0% -> 18%
where the time goes in v1:
time: 107 us; the launch traced here: 106 us
  starting transfers between devices  42.5 us (40%)
  Pallas kernels  27.9 us (26%)
  waiting for transfers between devices  26.9 us (25%)
  local copies, waits for them, and re-layouts  5.31 us (5%)
  other arithmetic  2.4 us (2%)
    ppermute x12, starting transfers between devices, on_device(): landed.append([lax.ppermute(payload, 'cols', pairs) for pairs in permutes])  34.9 us
    pallas_call x4, Pallas kernels, update(): pl.pallas_call(functools.partial(update_kernel, chunk, index, nrows, ncol...  25.8 us
    ppermute x12, waiting for transfers between devices, on_device(): landed.append([lax.ppermute(payload, 'cols', pairs) for pairs in permutes])  25.6 us
    ppermute x2, starting transfers between devices, down_rows(): x = jnp.where(row_device < 2 * reach, x, lax.ppermute(x, 'rows', hops))  7.45 us
    unnamed x17, local copies, waits for them, and re-layouts  5.28 us
  transfers between devices with their start and end apart: 16, of which 9 were waited for; matrix products, arithmetic and copies ran while one was open for 2% of the time, Pallas kernels for 18%

profile of v1, /device:TPU:0, one launch (start us, length us, event | category | flops | bytes accessed | tf_op | source)
XLA Modules:
  0.0 106.0 jit_solution(17509790558744435113)
XLA Ops:
  1.4 3.7 %copy-done = bf16[12,6,256,256]{3,2,1,0:T(8,128)(2,1)S(1)} copy-done((bf16[12,6,256,256]{3,2,1,0:T(8,128)(2,1)S(1)}, bf16[12,6,256,256]{3,2,1,0:T(8,128)(2,1)}, u32[]{:S(2)}) %copy-start) | copy-done | bytes 9437208
  5.9 1.6 %shard_map.59 = (bf16[4,784,256]{2,1,0:T(8,128)(2,1)S(1)}, bf16[1584,256]{1,0:T(8,128)(2,1)}) custom-call(s32[12,6]{1,0:T(8,128)S(1)} %copy.16.pattern.refs_0_, bf16[12,6,256,256]{3,2,1,0:T(8,128)(2,1)S(1)} %copy-done, bf16[12,6,256,256]{3,2,1,0:T(8,128)(2,1)S(1)} %copy-done, f32[12,3,256]{2,1,0:T(4,128)S(1)} %copy-done.6), custom_call_target="tpu_custom_call" | custom-call | tf_op jit(solution)/shard_map/pallas_call | solution.py:119
  7.5 3.0 %collective-permute-start.2 = (bf16[784,256]{1,0:T(8,128)(2,1)S(1)}, bf16[784,256]{1,0:T(8,128)(2,1)S(1)}, u32[]{:S(2)}, u32[]{:S(2)}) collective-permute-start(bf16[784,256]{1,0:T(8,128)(2,1)S(1)} %slice_bitcast_fusion), channel_id=1, source_target_pairs={{4,6},{5,7},{0,1},{1,0},{2,3},{3,2},{6,5},{7,4},{12,14},{13,15},{8... | collective-permute-start | bytes 1204232 | tf_op jit(solution)/shard_map/ppermute | solution.py:309
  10.5 4.6 %collective-permute-start.3 = (bf16[784,256]{1,0:T(8,128)(2,1)S(1)}, bf16[784,256]{1,0:T(8,128)(2,1)S(1)}, u32[]{:S(2)}, u32[]{:S(2)}) collective-permute-start(bf16[784,256]{1,0:T(8,128)(2,1)S(1)} %slice_bitcast_fusion), channel_id=1, source_target_pairs={{0,4},{1,5},{4,2},{5,3},{6,7},{7,6},{8,12},{9,13},{12,10},{13,11},... | collective-permute-start | bytes 1204232 | tf_op jit(solution)/shard_map/ppermute | solution.py:309
  15.2 4.7 %collective-permute-done.2.refs_11_ = bf16[784,256]{1,0:T(8,128)(2,1)S(1)} collective-permute-done((bf16[784,256]{1,0:T(8,128)(2,1)S(1)}, bf16[784,256]{1,0:T(8,128)(2,1)S(1)}, u32[]{:S(2)}, u32[]{:S(2)}) %collective-permute-start.2) | collective-permute-done | bytes 401440 | tf_op jit(solution)/shard_map/ppermute | solution.py:309
  19.8 3.5 %collective-permute-done.3.refs_9_ = bf16[784,256]{1,0:T(8,128)(2,1)S(1)} collective-permute-done((bf16[784,256]{1,0:T(8,128)(2,1)S(1)}, bf16[784,256]{1,0:T(8,128)(2,1)S(1)}, u32[]{:S(2)}, u32[]{:S(2)}) %collective-permute-start.3) | collective-permute-done | bytes 401440 | tf_op jit(solution)/shard_map/ppermute | solution.py:309
  23.4 1.6 %collective-permute-start.4 = (bf16[784,256]{1,0:T(8,128)(2,1)S(1)}, bf16[784,256]{1,0:T(8,128)(2,1)S(1)}, u32[]{:S(2)}, u32[]{:S(2)}) collective-permute-start(bf16[784,256]{1,0:T(8,128)(2,1)S(1)} %bitcast_select_fusion.2), channel_id=1, source_target_pairs={{4,6},{5,7},{0,1},{1,0},{2,3},{3,2},{6,5},{7,4},{12,14},{13,15},{8... | collective-permute-start | bytes 1204232 | tf_op jit(solution)/shard_map/ppermute | solution.py:309
  25.0 4.3 %collective-permute-start.5 = (bf16[784,256]{1,0:T(8,128)(2,1)S(1)}, bf16[784,256]{1,0:T(8,128)(2,1)S(1)}, u32[]{:S(2)}, u32[]{:S(2)}) collective-permute-start(bf16[784,256]{1,0:T(8,128)(2,1)S(1)} %bitcast_select_fusion.2), channel_id=1, source_target_pairs={{0,4},{1,5},{4,2},{5,3},{6,7},{7,6},{8,12},{9,13},{12,10},{13,11},... | collective-permute-start | bytes 1204232 | tf_op jit(solution)/shard_map/ppermute | solution.py:309
  29.3 4.3 %collective-permute-start = (bf16[1584,256]{1,0:T(8,128)(2,1)}, bf16[1584,256]{1,0:T(8,128)(2,1)}, u32[]{:S(2)}, u32[]{:S(2)}) collective-permute-start(bf16[1584,256]{1,0:T(8,128)(2,1)} %get-tuple-element.13), channel_id=1, source_target_pairs={{0,16},{8,24},{1,17},{9,25},{2,18},{10,26},{3,19},{11,27},{4,20},{... | collective-permute-start | bytes 2433032 | tf_op jit(solution)/shard_map/ppermute | solution.py:296
  33.6 2.7 %collective-permute-done.5.refs_8_.refs_9_ = bf16[784,256]{1,0:T(8,128)(2,1)S(1)} collective-permute-done((bf16[784,256]{1,0:T(8,128)(2,1)S(1)}, bf16[784,256]{1,0:T(8,128)(2,1)S(1)}, u32[]{:S(2)}, u32[]{:S(2)}) %collective-permute-start.5) | collective-permute-done | bytes 401440 | tf_op jit(solution)/shard_map/ppermute | solution.py:309
  37.2 5.3 %collective-permute-start.6 = (bf16[784,256]{1,0:T(8,128)(2,1)}, bf16[784,256]{1,0:T(8,128)(2,1)S(1)}, u32[]{:S(2)}, u32[]{:S(2)}) collective-permute-start(bf16[784,256]{1,0:T(8,128)(2,1)} %bitcast_select_fusion.1), channel_id=1, source_target_pairs={{0,4},{1,5},{4,2},{5,3},{6,7},{7,6},{8,12},{9,13},{12,10},{13,11},... | collective-permute-start | bytes 1204232 | tf_op jit(solution)/shard_map/ppermute | solution.py:309
  43.9 5.1 %collective-permute-done.6.refs_13_.refs_8_.refs_9_ = bf16[784,256]{1,0:T(8,128)(2,1)S(1)} collective-permute-done((bf16[784,256]{1,0:T(8,128)(2,1)}, bf16[784,256]{1,0:T(8,128)(2,1)S(1)}, u32[]{:S(2)}, u32[]{:S(2)}) %collective-permute-start.6) | collective-permute-done | bytes 401440 | tf_op jit(solution)/shard_map/ppermute | solution.py:309
  48.9 3.0 %collective-permute-done.7.refs_12_.refs_10_.refs_11_ = bf16[784,256]{1,0:T(8,128)(2,1)S(1)} collective-permute-done((bf16[784,256]{1,0:T(8,128)(2,1)}, bf16[784,256]{1,0:T(8,128)(2,1)S(1)}, u32[]{:S(2)}, u32[]{:S(2)}) %collective-permute-start.7) | collective-permute-done | bytes 401440 | tf_op jit(solution)/shard_map/ppermute | solution.py:309
  53.5 2.7 %collective-permute-start.11 = (bf16[784,256]{1,0:T(8,128)(2,1)S(1)}, bf16[784,256]{1,0:T(8,128)(2,1)S(1)}, u32[]{:S(2)}, u32[]{:S(2)}) collective-permute-start(bf16[784,256]{1,0:T(8,128)(2,1)S(1)} %bitcast_select_fusion), channel_id=1, source_target_pairs={{0,4},{1,5},{4,2},{5,3},{6,7},{7,6},{8,12},{9,13},{12,10},{13,11},... | collective-permute-start | bytes 1204232 | tf_op jit(solution)/shard_map/ppermute | solution.py:309
  57.7 3.1 %collective-permute-start.8 = (bf16[256,256]{1,0:T(8,128)(2,1)S(1)}, bf16[256,256]{1,0:T(8,128)(2,1)S(1)}, u32[]{:S(2)}, u32[]{:S(2)}) collective-permute-start(bf16[256,256]{1,0:T(8,128)(2,1)S(1)} %fusion.1), channel_id=1, source_target_pairs={{0,16},{8,24},{1,17},{9,25},{2,18},{10,26},{3,19},{11,27},{4,20},{... | collective-permute-start | bytes 393224 | tf_op jit(solution)/shard_map/ppermute | solution.py:296
  61.6 5.3 %collective-permute-start.12 = (bf16[784,256]{1,0:T(8,128)(2,1)S(1)}, bf16[784,256]{1,0:T(8,128)(2,1)S(1)}, u32[]{:S(2)}, u32[]{:S(2)}) collective-permute-start(bf16[784,256]{1,0:T(8,128)(2,1)S(1)} %broadcast_select_fusion.2), channel_id=1, source_target_pairs={{0,4},{1,5},{4,2},{5,3},{6,7},{7,6},{8,12},{9,13},{12,10},{13,11},... | collective-permute-start | bytes 1204232 | tf_op jit(solution)/shard_map/ppermute | solution.py:309
  66.9 1.5 %collective-permute-start.13 = (bf16[784,256]{1,0:T(8,128)(2,1)S(1)}, bf16[784,256]{1,0:T(8,128)(2,1)S(1)}, u32[]{:S(2)}, u32[]{:S(2)}) collective-permute-start(bf16[784,256]{1,0:T(8,128)(2,1)S(1)} %broadcast_select_fusion.2), channel_id=1, source_target_pairs={{4,6},{5,7},{0,1},{1,0},{2,3},{3,2},{6,5},{7,4},{12,14},{13,15},{8... | collective-permute-start | bytes 1204232 | tf_op jit(solution)/shard_map/ppermute | solution.py:309
  70.5 1.8 %collective-permute-done.12.refs_13_.refs_8_ = bf16[784,256]{1,0:T(8,128)(2,1)S(1)} collective-permute-done((bf16[784,256]{1,0:T(8,128)(2,1)S(1)}, bf16[784,256]{1,0:T(8,128)(2,1)S(1)}, u32[]{:S(2)}, u32[]{:S(2)}) %collective-permute-start.12) | collective-permute-done | bytes 401440 | tf_op jit(solution)/shard_map/ppermute | solution.py:309
  72.3 4.0 %collective-permute-done.13.refs_12_.refs_10_ = bf16[784,256]{1,0:T(8,128)(2,1)S(1)} collective-permute-done((bf16[784,256]{1,0:T(8,128)(2,1)S(1)}, bf16[784,256]{1,0:T(8,128)(2,1)S(1)}, u32[]{:S(2)}, u32[]{:S(2)}) %collective-permute-start.13) | collective-permute-done | bytes 401440 | tf_op jit(solution)/shard_map/ppermute | solution.py:309
  76.3 2.5 %collective-permute-start.14 = (bf16[784,256]{1,0:T(8,128)(2,1)S(1)}, bf16[784,256]{1,0:T(8,128)(2,1)S(1)}, u32[]{:S(2)}, u32[]{:S(2)}) collective-permute-start(bf16[784,256]{1,0:T(8,128)(2,1)S(1)} %broadcast_select_fusion.1), channel_id=1, source_target_pairs={{4,6},{5,7},{0,1},{1,0},{2,3},{3,2},{6,5},{7,4},{12,14},{13,15},{8... | collective-permute-start | bytes 1204232 | tf_op jit(solution)/shard_map/ppermute | solution.py:309
  80.1 6.5 %shard_map.61 = (bf16[12,6,256,256]{3,2,1,0:T(8,128)(2,1)}, f32[12,3,256]{2,1,0:T(4,128)}) custom-call(s32[12,6]{1,0:T(8,128)S(1)} %copy.16.pattern.refs_0_, bf16[12,6,256,256]{3,2,1,0:T(8,128)(2,1)} %refs_1_.7, f32[12,3,256]{2,1,0:T(4,128)S(1)} %copy-done.7, bf16[6,512,256]{2,1,0:T(8,128)(2,1)S(1)} %get-tuple-element.15.refs_3_, ...), custom_call_target="tpu_custom_call" | custom-call | flops 1610612736 | bytes 6291456 | tf_op jit(solution)/shard_map/pallas_call | solution.py:255
  86.6 6.7 %shard_map.62 = (bf16[12,6,256,256]{3,2,1,0:T(8,128)(2,1)}, f32[12,3,256]{2,1,0:T(4,128)}) custom-call(s32[12,6]{1,0:T(8,128)S(1)} %copy.16.pattern.refs_0_, bf16[12,6,256,256]{3,2,1,0:T(8,128)(2,1)} %refs_1_.7, f32[12,3,256]{2,1,0:T(4,128)S(1)} %copy-done.7, ...), custom_call_target="tpu_custom_call", output_to_operand_aliasing={{0}: (14, {}), {1}: (15, {})} | custom-call | flops 1610612736 | bytes 6291456 | tf_op jit(solution)/shard_map/pallas_call | solution.py:255
  93.4 5.9 %shard_map.63 = (bf16[12,6,256,256]{3,2,1,0:T(8,128)(2,1)}, f32[12,3,256]{2,1,0:T(4,128)}) custom-call(s32[12,6]{1,0:T(8,128)S(1)} %copy.16.pattern.refs_0_, bf16[12,6,256,256]{3,2,1,0:T(8,128)(2,1)} %refs_1_.7, f32[12,3,256]{2,1,0:T(4,128)S(1)} %copy-done.7, ...), custom_call_target="tpu_custom_call", output_to_operand_aliasing={{0}: (14, {}), {1}: (15, {})} | custom-call | flops 1610612736 | bytes 6291456 | tf_op jit(solution)/shard_map/pallas_call | solution.py:255
  99.2 6.7 %shard_map.64 = (bf16[12,6,256,256]{3,2,1,0:T(8,128)(2,1)}, f32[12,3,256]{2,1,0:T(4,128)}) custom-call(s32[12,6]{1,0:T(8,128)S(1)} %copy.16.pattern.refs_0_, bf16[12,6,256,256]{3,2,1,0:T(8,128)(2,1)} %refs_1_.7, f32[12,3,256]{2,1,0:T(4,128)S(1)} %copy-done.7, ...), custom_call_target="tpu_custom_call", output_to_operand_aliasing={{0}: (14, {}), {1}: (15, {})} | custom-call | flops 1610612736 | bytes 6291456 | tf_op jit(solution)/shard_map/pallas_call | solution.py:255
  (40 shorter events, 11.0 us)
Async XLA Ops:
  1.4 3.7 %copy-start = (bf16[12,6,256,256]{3,2,1,0:T(8,128)(2,1)S(1)}, bf16[12,6,256,256]{3,2,1,0:T(8,128)(2,1)}, u32[]{:S(2)}) copy-start(bf16[12,6,256,256]{3,2,1,0:T(8,128)(2,1)} %refs_1_.7) | copy-start | bytes 28311556
  5.1 0.8 copy-start.6
  7.5 12.3 %collective-permute-start.2 = (bf16[784,256]{1,0:T(8,128)(2,1)S(1)}, bf16[784,256]{1,0:T(8,128)(2,1)S(1)}, u32[]{:S(2)}, u32[]{:S(2)}) collective-permute-start(bf16[784,256]{1,0:T(8,128)(2,1)S(1)} %slice_bitcast_fusion), channel_id=1, source_target_pairs={{4,6},{5,7},{0,1},{1,0},{2,3},{3,2},{6,5},{7,4},{12,14},{13,15},{8... | collective-permute-start | bytes 1204232 | tf_op jit(solution)/shard_map/ppermute | solution.py:309
  10.5 12.8 %collective-permute-start.3 = (bf16[784,256]{1,0:T(8,128)(2,1)S(1)}, bf16[784,256]{1,0:T(8,128)(2,1)S(1)}, u32[]{:S(2)}, u32[]{:S(2)}) collective-permute-start(bf16[784,256]{1,0:T(8,128)(2,1)S(1)} %slice_bitcast_fusion), channel_id=1, source_target_pairs={{0,4},{1,5},{4,2},{5,3},{6,7},{7,6},{8,12},{9,13},{12,10},{13,11},... | collective-permute-start | bytes 1204232 | tf_op jit(solution)/shard_map/ppermute | solution.py:309
  19.8 16.5 %copy-start.2 = (bf16[784,256]{1,0:T(8,128)(2,1)}, bf16[784,256]{1,0:T(8,128)(2,1)S(1)}, u32[]{:S(2)}) copy-start(bf16[784,256]{1,0:T(8,128)(2,1)S(1)} %collective-permute-done.2.refs_11_) | copy-start | bytes 1204228
  23.4 13.8 %copy-start.4 = (bf16[784,256]{1,0:T(8,128)(2,1)}, bf16[784,256]{1,0:T(8,128)(2,1)S(1)}, u32[]{:S(2)}) copy-start(bf16[784,256]{1,0:T(8,128)(2,1)S(1)} %collective-permute-done.3.refs_9_) | copy-start | bytes 1204228
  23.4 10.2 %collective-permute-start.4 = (bf16[784,256]{1,0:T(8,128)(2,1)S(1)}, bf16[784,256]{1,0:T(8,128)(2,1)S(1)}, u32[]{:S(2)}, u32[]{:S(2)}) collective-permute-start(bf16[784,256]{1,0:T(8,128)(2,1)S(1)} %bitcast_select_fusion.2), channel_id=1, source_target_pairs={{4,6},{5,7},{0,1},{1,0},{2,3},{3,2},{6,5},{7,4},{12,14},{13,15},{8... | collective-permute-start | bytes 1204232 | tf_op jit(solution)/shard_map/ppermute | solution.py:309
  25.0 11.4 %collective-permute-start.5 = (bf16[784,256]{1,0:T(8,128)(2,1)S(1)}, bf16[784,256]{1,0:T(8,128)(2,1)S(1)}, u32[]{:S(2)}, u32[]{:S(2)}) collective-permute-start(bf16[784,256]{1,0:T(8,128)(2,1)S(1)} %bitcast_select_fusion.2), channel_id=1, source_target_pairs={{0,4},{1,5},{4,2},{5,3},{6,7},{7,6},{8,12},{9,13},{12,10},{13,11},... | collective-permute-start | bytes 1204232 | tf_op jit(solution)/shard_map/ppermute | solution.py:309
  29.3 26.9 %collective-permute-start = (bf16[1584,256]{1,0:T(8,128)(2,1)}, bf16[1584,256]{1,0:T(8,128)(2,1)}, u32[]{:S(2)}, u32[]{:S(2)}) collective-permute-start(bf16[1584,256]{1,0:T(8,128)(2,1)} %get-tuple-element.13), channel_id=1, source_target_pairs={{0,16},{8,24},{1,17},{9,25},{2,18},{10,26},{3,19},{11,27},{4,20},{... | collective-permute-start | bytes 2433032 | tf_op jit(solution)/shard_map/ppermute | solution.py:296
  37.2 11.7 %collective-permute-start.6 = (bf16[784,256]{1,0:T(8,128)(2,1)}, bf16[784,256]{1,0:T(8,128)(2,1)S(1)}, u32[]{:S(2)}, u32[]{:S(2)}) collective-permute-start(bf16[784,256]{1,0:T(8,128)(2,1)} %bitcast_select_fusion.1), channel_id=1, source_target_pairs={{0,4},{1,5},{4,2},{5,3},{6,7},{7,6},{8,12},{9,13},{12,10},{13,11},... | collective-permute-start | bytes 1204232 | tf_op jit(solution)/shard_map/ppermute | solution.py:309
  42.5 9.4 %collective-permute-start.7 = (bf16[784,256]{1,0:T(8,128)(2,1)}, bf16[784,256]{1,0:T(8,128)(2,1)S(1)}, u32[]{:S(2)}, u32[]{:S(2)}) collective-permute-start(bf16[784,256]{1,0:T(8,128)(2,1)} %bitcast_select_fusion.1), channel_id=1, source_target_pairs={{4,6},{5,7},{0,1},{1,0},{2,3},{3,2},{6,5},{7,4},{12,14},{13,15},{8... | collective-permute-start | bytes 1204232 | tf_op jit(solution)/shard_map/ppermute | solution.py:309
  52.0 5.6 %copy-start.3 = (bf16[784,256]{1,0:T(8,128)(2,1)S(1)}, bf16[784,256]{1,0:T(8,128)(2,1)}, u32[]{:S(2)}) copy-start(bf16[784,256]{1,0:T(8,128)(2,1)} %copy-done.2) | copy-start | bytes 1204228
  52.0 5.6 %copy-start.5 = (bf16[784,256]{1,0:T(8,128)(2,1)S(1)}, bf16[784,256]{1,0:T(8,128)(2,1)}, u32[]{:S(2)}) copy-start(bf16[784,256]{1,0:T(8,128)(2,1)} %copy-done.4) | copy-start | bytes 1204228
  52.0 8.8 %collective-permute-start.10 = (bf16[784,256]{1,0:T(8,128)(2,1)S(1)}, bf16[784,256]{1,0:T(8,128)(2,1)S(1)}, u32[]{:S(2)}, u32[]{:S(2)}) collective-permute-start(bf16[784,256]{1,0:T(8,128)(2,1)S(1)} %bitcast_select_fusion), channel_id=1, source_target_pairs={{4,6},{5,7},{0,1},{1,0},{2,3},{3,2},{6,5},{7,4},{12,14},{13,15},{8... | collective-permute-start | bytes 1204232 | tf_op jit(solution)/shard_map/ppermute | solution.py:309
  53.5 8.0 %collective-permute-start.11 = (bf16[784,256]{1,0:T(8,128)(2,1)S(1)}, bf16[784,256]{1,0:T(8,128)(2,1)S(1)}, u32[]{:S(2)}, u32[]{:S(2)}) collective-permute-start(bf16[784,256]{1,0:T(8,128)(2,1)S(1)} %bitcast_select_fusion), channel_id=1, source_target_pairs={{0,4},{1,5},{4,2},{5,3},{6,7},{7,6},{8,12},{9,13},{12,10},{13,11},... | collective-permute-start | bytes 1204232 | tf_op jit(solution)/shard_map/ppermute | solution.py:309
  57.5 12.4 %copy-start.1 = (bf16[2,256,256]{2,1,0:T(8,128)(2,1)S(1)}, bf16[2,256,256]{2,1,0:T(8,128)(2,1)}, u32[]{:S(2)}) copy-start(bf16[2,256,256]{2,1,0:T(8,128)(2,1)} %refs_6_.7) | copy-start | bytes 786436
  57.5 12.4 %collective-permute-start.1 = (bf16[1584,256]{1,0:T(8,128)(2,1)S(1)}, bf16[1584,256]{1,0:T(8,128)(2,1)S(1)}, u32[]{:S(2)}, u32[]{:S(2)}) collective-permute-start(bf16[1584,256]{1,0:T(8,128)(2,1)S(1)} %broadcast_select_fusion.mine), channel_id=1, source_target_pairs={{0,8},{8,0},{16,24},{24,16},{1,9},{9,1},{17,25},{25,17},{2,10},{10... | collective-permute-start | bytes 2433032 | tf_op jit(solution)/shard_map/ppermute | solution.py:298
  57.7 10.8 %collective-permute-start.8 = (bf16[256,256]{1,0:T(8,128)(2,1)S(1)}, bf16[256,256]{1,0:T(8,128)(2,1)S(1)}, u32[]{:S(2)}, u32[]{:S(2)}) collective-permute-start(bf16[256,256]{1,0:T(8,128)(2,1)S(1)} %fusion.1), channel_id=1, source_target_pairs={{0,16},{8,24},{1,17},{9,25},{2,18},{10,26},{3,19},{11,27},{4,20},{... | collective-permute-start | bytes 393224 | tf_op jit(solution)/shard_map/ppermute | solution.py:296
  61.6 10.7 %collective-permute-start.12 = (bf16[784,256]{1,0:T(8,128)(2,1)S(1)}, bf16[784,256]{1,0:T(8,128)(2,1)S(1)}, u32[]{:S(2)}, u32[]{:S(2)}) collective-permute-start(bf16[784,256]{1,0:T(8,128)(2,1)S(1)} %broadcast_select_fusion.2), channel_id=1, source_target_pairs={{0,4},{1,5},{4,2},{5,3},{6,7},{7,6},{8,12},{9,13},{12,10},{13,11},... | collective-permute-start | bytes 1204232 | tf_op jit(solution)/shard_map/ppermute | solution.py:309
  66.9 9.4 %collective-permute-start.13 = (bf16[784,256]{1,0:T(8,128)(2,1)S(1)}, bf16[784,256]{1,0:T(8,128)(2,1)S(1)}, u32[]{:S(2)}, u32[]{:S(2)}) collective-permute-start(bf16[784,256]{1,0:T(8,128)(2,1)S(1)} %broadcast_select_fusion.2), channel_id=1, source_target_pairs={{4,6},{5,7},{0,1},{1,0},{2,3},{3,2},{6,5},{7,4},{12,14},{13,15},{8... | collective-permute-start | bytes 1204232 | tf_op jit(solution)/shard_map/ppermute | solution.py:309
  68.5 11.6 %copy-start.7 = (f32[12,3,256]{2,1,0:T(4,128)S(1)}, f32[12,3,256]{2,1,0:T(4,128)}, u32[]{:S(2)}) copy-start(f32[12,3,256]{2,1,0:T(4,128)} %refs_2_.7) | copy-start | bytes 110596
  68.5 1.4 %collective-permute-start.9 = (bf16[256,256]{1,0:T(8,128)(2,1)S(1)}, bf16[256,256]{1,0:T(8,128)(2,1)S(1)}, u32[]{:S(2)}, u32[]{:S(2)}) collective-permute-start(bf16[256,256]{1,0:T(8,128)(2,1)S(1)} %broadcast_select_fusion.3.corner), channel_id=1, source_target_pairs={{0,8},{8,0},{16,24},{24,16},{1,9},{9,1},{17,25},{25,17},{2,10},{10... | collective-permute-start | bytes 393224 | tf_op jit(solution)/shard_map/ppermute | solution.py:298
  76.3 22.9 %collective-permute-start.14 = (bf16[784,256]{1,0:T(8,128)(2,1)S(1)}, bf16[784,256]{1,0:T(8,128)(2,1)S(1)}, u32[]{:S(2)}, u32[]{:S(2)}) collective-permute-start(bf16[784,256]{1,0:T(8,128)(2,1)S(1)} %broadcast_select_fusion.1), channel_id=1, source_target_pairs={{4,6},{5,7},{0,1},{1,0},{2,3},{3,2},{6,5},{7,4},{12,14},{13,15},{8... | collective-permute-start | bytes 1204232 | tf_op jit(solution)/shard_map/ppermute | solution.py:309
  78.8 20.4 %collective-permute-start.15 = (bf16[784,256]{1,0:T(8,128)(2,1)S(1)}, bf16[784,256]{1,0:T(8,128)(2,1)S(1)}, u32[]{:S(2)}, u32[]{:S(2)}) collective-permute-start(bf16[784,256]{1,0:T(8,128)(2,1)S(1)} %broadcast_select_fusion.1), channel_id=1, source_target_pairs={{0,4},{1,5},{4,2},{5,3},{6,7},{7,6},{8,12},{9,13},{12,10},{13,11},... | collective-permute-start | bytes 1204232 | tf_op jit(solution)/shard_map/ppermute | solution.py:309

commit v2 on v1

--- a/solution.py
+++ b/solution.py
@@ -12,7 +12,10 @@
 FLAG_ROWS = 16
 PIECE_ROWS = 32
 MOST_CHUNKS = 4
-VMEM_LIMIT = 40 * 1024 * 1024
+WIDE_VMEM = 56 * 1024 * 1024
+VMEM_LIMIT = 20 * 1024 * 1024
+EARLY_VMEM = 44 * 1024 * 1024
+LATE_VMEM = 52 * 1024 * 1024
 
 
 def broadcast_plan(groups):
@@ -91,20 +94,21 @@
     return (x[0:8] + x[8:16] + x[16:24])[:n]
 
 
-def prepare_kernel(chunk, pattern, column, row, rhs, column_out, row_out):
+def prepare_kernel(chunk, pattern, column, row, rhs, *outs):
+    *column_out, row_out = outs
     rows, width = column.shape[0], column.shape[-1]
     cols = row.shape[1]
     lines = lax.broadcasted_iota(jnp.int32, (FLAG_ROWS, width), 0)
     for k in range(rows // chunk):
         flags = jnp.zeros((FLAG_ROWS, width), F32)
         for i in range(chunk):
-            live = pattern[k * chunk + i, 0] == 1
-            column_out[k, i * width : (i + 1) * width] = jnp.where(live, column[k * chunk + i, 0], jnp.zeros((), BF))
+            live = pattern[0, k * chunk + i] == 1
+            column_out[k][i * width : (i + 1) * width] = jnp.where(live, column[k * chunk + i, 0], jnp.zeros((), BF))
             flags = jnp.where((lines == i) & live, 1.0, flags)
-        column_out[k, chunk * width : chunk * width + FLAG_ROWS] = flags.astype(BF)
+        column_out[k][chunk * width : chunk * width + FLAG_ROWS] = flags.astype(BF)
     flags = jnp.zeros((FLAG_ROWS, width), F32)
     for j in range(cols):
-        live = pattern[0, j] == 1
+        live = pattern[j, 0] == 1
         row_out[j * width : (j + 1) * width] = jnp.where(live, row[0, j], jnp.zeros((), BF))
         flags = jnp.where((lines == j) & live, 1.0, flags)
     base = cols * width
@@ -115,7 +119,8 @@
 def prepare(blocks, pattern, right_sides, chunk):
     rows, cols, width, _ = blocks.shape
     dirs = right_sides.shape[1]
-    n = rows // chunk
+    shapes = [(chunk * width + FLAG_ROWS, width)] * (rows // chunk)
+    shapes.append((cols * width + FLAG_ROWS + PIECE_ROWS, width))
     return pl.pallas_call(
         functools.partial(prepare_kernel, chunk),
         grid=(1,),
@@ -125,21 +130,15 @@
             pl.BlockSpec((1, cols, width, width), lambda s: (0, 0, 0, 0)),
             pl.BlockSpec((1, dirs, width), lambda s: (0, 0, 0)),
         ],
-        out_specs=[
-            pl.BlockSpec((n, chunk * width + FLAG_ROWS, width), lambda s: (0, 0, 0)),
-            pl.BlockSpec((cols * width + FLAG_ROWS + PIECE_ROWS, width), lambda s: (0, 0)),
-        ],
-        out_shape=[
-            jax.ShapeDtypeStruct((n, chunk * width + FLAG_ROWS, width), BF),
-            jax.ShapeDtypeStruct((cols * width + FLAG_ROWS + PIECE_ROWS, width), BF),
-        ],
-        compiler_params=pltpu.CompilerParams(vmem_limit_bytes=VMEM_LIMIT),
+        out_specs=[pl.BlockSpec(shape, lambda s: (0, 0)) for shape in shapes],
+        out_shape=[jax.ShapeDtypeStruct(shape, BF) for shape in shapes],
+        compiler_params=pltpu.CompilerParams(vmem_limit_bytes=WIDE_VMEM),
     )(pattern, blocks, blocks, right_sides)
 
 
 def panel_kernel(dirs, ncols, mine, other, corner, other_corner, inverse, upper, upper_one, sides):
     width = inverse.shape[-1]
-    cols = upper.shape[0]
+    cols = upper.shape[1] // width
     even = lax.axis_index("rows") % 2 == 0
     col = lax.axis_index("cols")
 
@@ -157,8 +156,9 @@
         zeroth = jnp.where(j * ncols + col > 0, zeroth, zero)
         fresh = (first.astype(F32) - dot(lower_one, zeroth)).astype(BF)
         keep = (flags[j : j + 1] > 0.5) & (j * ncols + col > 1)
-        upper[j, 0:width] = zeroth
-        upper[j, width : 2 * width] = jnp.where(keep, fresh, zero)
+        at = slice(j * width, (j + 1) * width)
+        upper[0:width, at] = zeroth
+        upper[width : 2 * width, at] = jnp.where(keep, fresh, zero)
     side_zero, side_one = pick(base + FLAG_ROWS, base + FLAG_ROWS + PIECE_ROWS)
     sides[0] = side_zero
     later = sum_pieces(side_one.astype(F32), dirs) - sum_pieces(dot_t(side_zero, lower_one), dirs)
@@ -170,7 +170,7 @@
     return pl.pallas_call(
         functools.partial(panel_kernel, dirs, ncols),
         out_shape=[
-            jax.ShapeDtypeStruct((cols, 2 * width, width), BF),
+            jax.ShapeDtypeStruct((2 * width, cols * width), BF),
             jax.ShapeDtypeStruct((width, width), BF),
             jax.ShapeDtypeStruct((2, PIECE_ROWS, width), BF),
         ],
@@ -181,93 +181,103 @@
     )(mine, other, corner, other_corner, inverse)
 
 
-def update_kernel(chunk, index, nrows, ncols, sources, n_refs, aliased, *refs):
+def update_kernel(chunk, first_chunk, nrows, ncols, sources, n_refs, aliased, *refs):
     pattern, blocks, rhs, upper, upper_one, sides, inverse = refs[:7]
     landed = refs[7 : 7 + n_refs]
-    out, forward, columns, sems = refs[7 + n_refs + aliased :]
+    out, forward, columns, lower, work, in_sems, out_sems = refs[7 + n_refs + aliased :]
     width = inverse.shape[-1]
-    cols = blocks.shape[1]
+    count, cols = work.shape[:2]
     row_device, col = lax.axis_index("rows"), lax.axis_index("cols")
     pair, side = col // 2, col % 2
-    step = pl.program_id(0)
-
-    @pl.when(step == 0)
-    def _():
+    zero = jnp.zeros((), BF)
+    base = first_chunk * chunk
+    tall = chunk * width
+
+    def fetch(i):
+        return pltpu.make_async_copy(blocks.at[base + i], work.at[i], in_sems.at[i])
+
+    def send(i):
+        return pltpu.make_async_copy(work.at[i], out.at[base + i], out_sems.at[i])
+
+    @pl.loop(0, count)
+    def _(i):
+        fetch(i).start()
+
+    for k, per_chunk in enumerate(sources):
         for which in (0, 1):
-            for ref, pairs in sources[which]:
+            for ref, pairs in per_chunk[which]:
                 hit = functools.reduce(jnp.logical_or, [pair == g for g in pairs])
-                source = landed[ref[0]] if ref[1] is None else landed[ref[0]].at[ref[1]]
 
                 @pl.when(hit)
-                def _(source=source, which=which):
-                    place = side if which == 0 else 1 - side
-                    pltpu.make_async_copy(source, columns.at[place], sems.at[which]).start()
-
-        for which in (0, 1):
-            pltpu.make_async_copy(columns.at[which], columns.at[which], sems.at[which]).wait()
-
-    local = index * chunk + step
-    here = local * nrows + row_device
-    zero = jnp.zeros((), BF)
-    at = pl.ds(pl.multiple_of(step * width, width), width)
-    lower_zero = dot(columns[0, at], inverse[0]).astype(BF)
-    lower_zero = jnp.where(here > 0, lower_zero, zero)
-    flags = columns[1, chunk * width : chunk * width + FLAG_ROWS].astype(F32)
-    lines = lax.broadcasted_iota(jnp.int32, flags.shape, 0)
-    live = jnp.sum(jnp.where(lines == step, flags, 0.0), 0, keepdims=True) > 0.5
-    pivot = (columns[1, at].astype(F32) - dot(lower_zero, upper_one[...])).astype(BF)
-    lower_one = dot(jnp.where(live, pivot, zero), inverse[1]).astype(BF)
-    lower_one = jnp.where(here > 1, lower_one, zero)
-    lower = jnp.concatenate([lower_zero, lower_one], 1)
-    for j in range(cols):
-        keep = pattern[local, j] == 1
-
-        @pl.when(keep)
-        def _(j=j):
-            out[0, j] = (blocks[0, j].astype(F32) - dot(lower, upper[j])).astype(BF)
-
-        @pl.when(jnp.logical_not(keep))
-        def _(j=j):
-            out[0, j] = jnp.zeros((width, width), BF)
-
-    @pl.when((col == 0) & (here > 0))
-    def _():
-        out[0, 0] = lower_zero
-
-    @pl.when((col == 1) & (here > 1))
-    def _():
-        out[0, 0] = lower_one
-
-    dirs = rhs.shape[1]
-    first = rhs[0] - sum_pieces(dot_t(sides[0], lower_zero), dirs)
-    forward[0] = first - sum_pieces(dot_t(sides[1], lower_one), dirs)
-
-
-def update(chunk, index, nrows, ncols, sources, landed, pattern, blocks, rhs, upper, upper_one, sides, inverse, before):
+                def _(source=landed[ref], which=which, k=k):
+                    columns[k, side if which == 0 else 1 - side] = source[...]
+
+    @pl.loop(0, len(sources))
+    def _(k):
+        start = (base + k * chunk) * nrows + row_device
+        glob = start + nrows * (lax.broadcasted_iota(jnp.int32, (tall, 1), 0) // width)
+        lower_zero = jnp.where(glob > 0, dot(columns[k, 0, 0:tall], inverse[0]), 0.0).astype(BF)
+        lower[k, :, 0:width] = lower_zero
+        pivot = (columns[k, 1, 0:tall].astype(F32) - dot(lower_zero, upper_one[...])).astype(BF)
+        flags = columns[k, 1, tall : tall + FLAG_ROWS].astype(F32)
+        kept = [jnp.where(flags[i : i + 1] > 0.5, pivot[i * width : (i + 1) * width], zero) for i in range(chunk)]
+        lower_one = dot(jnp.concatenate(kept, 0), inverse[1])
+        lower[k, :, width : 2 * width] = jnp.where(glob > 1, lower_one, 0.0).astype(BF)
+
+    @pl.loop(0, count)
+    def _(i):
+        k, at = i // chunk, pl.ds(pl.multiple_of((i % chunk) * width, width), width)
+        glob = (base + i) * nrows + row_device
+        fetch(i).wait()
+        change = dot(lower[k, at], upper[...])
+        for j in range(cols):
+            fresh = (work[i, j].astype(F32) - change[:, j * width : (j + 1) * width]).astype(BF)
+            work[i, j] = jnp.where(pattern[j, base + i] == 1, fresh, zero)
+
+        @pl.when((col == 0) & (glob > 0))
+        def _():
+            work[i, 0] = lower[k, at, 0:width]
+
+        @pl.when((col == 1) & (glob > 1))
+        def _():
+            work[i, 0] = lower[k, at, width : 2 * width]
+
+        send(i).start()
+        dirs = rhs.shape[1]
+        first = rhs[base + i] - sum_pieces(dot_t(sides[0], lower[k, at, 0:width]), dirs)
+        forward[i] = first - sum_pieces(dot_t(sides[1], lower[k, at, width : 2 * width]), dirs)
+
+    @pl.loop(0, count)
+    def _(i):
+        send(i).wait()
+
+
+def update(
+    chunk, first_chunk, nrows, ncols, sources, landed, pattern, blocks, rhs, upper, upper_one, sides, inverse, before, limit
+):
     rows, cols, width, _ = blocks.shape
     dirs = rhs.shape[1]
-    aliased = 0 if before is None else 2
-    whole = pl.BlockSpec(memory_space=pltpu.VMEM)
+    aliased = 0 if before is None else 1
     far = pl.BlockSpec(memory_space=pl.ANY)
-    block_spec = pl.BlockSpec((1, cols, width, width), lambda s: (index * chunk + s, 0, 0, 0))
-    rhs_spec = pl.BlockSpec((1, dirs, width), lambda s: (index * chunk + s, 0, 0))
+    near = pl.BlockSpec(memory_space=pltpu.VMEM)
+    count = chunk * len(sources)
     n_in = 7 + len(landed)
     return pl.pallas_call(
-        functools.partial(update_kernel, chunk, index, nrows, ncols, sources, len(landed), aliased),
-        grid=(chunk,),
-        in_specs=[pl.BlockSpec(memory_space=pltpu.SMEM), block_spec, rhs_spec]
-        + [whole] * 4
-        + [far] * (len(landed) + aliased),
-        out_specs=[block_spec, rhs_spec],
-        out_shape=[jax.ShapeDtypeStruct(blocks.shape, BF), jax.ShapeDtypeStruct(rhs.shape, F32)],
+        functools.partial(update_kernel, chunk, first_chunk, nrows, ncols, sources, len(landed), aliased),
+        in_specs=[pl.BlockSpec(memory_space=pltpu.SMEM), far] + [near] * (5 + len(landed)) + [far] * aliased,
+        out_specs=[far, near],
+        out_shape=[jax.ShapeDtypeStruct(blocks.shape, BF), jax.ShapeDtypeStruct((count, dirs, width), F32)],
         scratch_shapes=[
-            pltpu.VMEM((2, chunk * width + FLAG_ROWS, width), BF),
-            pltpu.SemaphoreType.DMA((2,)),
+            pltpu.VMEM((len(sources), 2, chunk * width + FLAG_ROWS, width), BF),
+            pltpu.VMEM((len(sources), chunk * width, 2 * width), BF),
+            pltpu.VMEM((count, cols, width, width), BF),
+            pltpu.SemaphoreType.DMA((count,)),
+            pltpu.SemaphoreType.DMA((count,)),
         ],
-        input_output_aliases={n_in: 0, n_in + 1: 1} if aliased else {},
-        compiler_params=pltpu.CompilerParams(vmem_limit_bytes=VMEM_LIMIT),
+        input_output_aliases={n_in: 0} if aliased else {},
+        compiler_params=pltpu.CompilerParams(vmem_limit_bytes=limit),
         cost_estimate=pl.CostEstimate(
-            flops=4 * chunk * (cols + 2) * width**3, bytes_accessed=4 * chunk * (cols + 2) * width**2, transcendentals=0
+            flops=4 * count * (cols + 2) * width**3, bytes_accessed=4 * count * (cols + 2) * width**2, transcendentals=0
         ),
     )(pattern, blocks, rhs, upper, upper_one, sides, inverse, *landed, *(before or ()))
 
@@ -284,7 +294,8 @@
     depth, own_from, other_depth, other_from, permutes = broadcast_plan(groups)
     n = max(d for d in range(1, MOST_CHUNKS + 1) if rows % d == 0)
     chunk = rows // n
-    columns, row = prepare(blocks, pattern, right_sides, chunk)
+    pattern = pattern.T
+    *columns, row = prepare(blocks, pattern, right_sides, chunk)
 
     def among(members):
         return functools.reduce(jnp.logical_or, [pair == g for g in members])
@@ -322,7 +333,7 @@
         return landed[key[1]][key[0]]
 
     own, cross = places(0)
-    mine_first = columns[0, :width]
+    mine_first = columns[0][:width]
     for key, members in own.items():
         if key != ("here",):
             mine_first = jnp.where(among(members), array_at(key)[:width], mine_first)
@@ -334,23 +345,24 @@
     corner, other_corner = down_rows(corner)
     upper, upper_one, sides = panel(dirs, cols, ncols, mine, other, corner, other_corner, pivot_inverse)
 
-    before = None
-    for k in range(n):
-        arrays, sources = [columns], []
-        for which in places(k):
-            found = []
-            for key, members in which.items():
-                if key == ("here",):
-                    found.append(((0, k), members))
-                else:
-                    arrays.append(array_at(key))
-                    found.append(((len(arrays) - 1, None), members))
-            sources.append(found)
-        before = update(
-            chunk, k, nrows, ncols, sources, arrays, pattern, blocks, right_sides, upper, upper_one, sides,
-            pivot_inverse, before,
-        )
-    return tuple(before)
+    out, forward = None, []
+    for first_chunk, last_chunk, limit in ((0, n - 1, EARLY_VMEM), (n - 1, n, LATE_VMEM)):
+        arrays, sources = [], []
+        for k in range(first_chunk, last_chunk):
+            sources.append([])
+            for which in places(k):
+                found = []
+                for key, members in which.items():
+                    found.append((len(arrays), members))
+                    arrays.append(columns[k] if key == ("here",) else array_at(key))
+                sources[-1].append(found)
+        if sources:
+            out, part = update(
+                chunk, first_chunk, nrows, ncols, sources, arrays, pattern, blocks, right_sides, upper, upper_one, sides,
+                pivot_inverse, None if out is None else (out,), limit,
+            )
+            forward.append(part)
+    return out, jnp.concatenate(forward, 0)
 
 
 def solution(mesh):

time: 107 us -> 94.8 us (0.89)
  Pallas kernels: 27.9 us -> 20.4 us
  other arithmetic: 2.4 us -> 6.92 us
  local copies, waits for them, and re-layouts: 5.31 us -> 0.9 us
  starting transfers between devices: 42.5 us -> 38.4 us
    pallas_call x4 -> x2, Pallas kernels: 25.8 us -> 16.7 us  [update(): pl.pallas_call(functools.partial(update_kernel, chunk, first_chunk, nrows...]
    ppermute x12, starting transfers between devices: 34.9 us -> 30.4 us  [on_device(): landed.append([lax.ppermute(payload, 'cols', pairs) for pairs in permutes])]
    unnamed x17 -> x24, local copies, waits for them, and re-layouts: 5.28 us -> 0.9 us
    select_n x3, other arithmetic: 0.99 us -> 3.98 us  [on_device(): payload = moved if payload is None else jnp.where(pair == 0, payload, moved)]
    pallas_call x1, Pallas kernels: 1.61 us -> 3.19 us  [prepare(): pl.pallas_call(functools.partial(prepare_kernel, chunk), grid=(1,), in_sp...]
  transfers between devices with their start and end apart: 16 -> 16, of which waited for: 9 -> 10; matrix products, arithmetic and copies ran while one was open for 2% -> 5% of each run, Pallas kernels for 18% -> 12%
where the time goes in v2:
time: 94.8 us; the launch traced here: 94.3 us
  starting transfers between devices  38.4 us (41%)
  waiting for transfers between devices  26.7 us (28%)
  Pallas kernels  20.4 us (22%)
  other arithmetic  6.92 us (7%)
    ppermute x12, starting transfers between devices, on_device(): landed.append([lax.ppermute(payload, 'cols', pairs) for pairs in permutes])  30.4 us
    ppermute x12, waiting for transfers between devices, on_device(): landed.append([lax.ppermute(payload, 'cols', pairs) for pairs in permutes])  25.4 us
    pallas_call x2, Pallas kernels, update(): pl.pallas_call(functools.partial(update_kernel, chunk, first_chunk, nrows...  16.7 us
    ppermute x2, starting transfers between devices, down_rows(): x = jnp.where(row_device < 2 * reach, x, lax.ppermute(x, 'rows', hops))  7.82 us
    select_n x3, other arithmetic, on_device(): payload = moved if payload is None else jnp.where(pair == 0, payload, moved)  3.98 us
    pallas_call x1, Pallas kernels, prepare(): pl.pallas_call(functools.partial(prepare_kernel, chunk), grid=(1,), in_sp...  3.19 us
  transfers between devices with their start and end apart: 16, of which 10 were waited for; matrix products, arithmetic and copies ran while one was open for 5% of the time, Pallas kernels for 12%

profile of v2, /device:TPU:0, one launch (start us, length us, event | category | flops | bytes accessed | tf_op | source)
XLA Modules:
  0.0 94.3 jit_solution(17151536301206724334)
XLA Ops:
  0.6 3.2 %shard_map.59 = (bf16[784,256]{1,0:T(8,128)(2,1)}, bf16[784,256]{1,0:T(8,128)(2,1)}, bf16[784,256]{1,0:T(8,128)(2,1)}, bf16[784,256]{1,0:T(8,128)(2,1)}, bf16[1584,256]{1,0:T(8,128)(2,1)}) custom-call(s32[6,12]{1,0:T(8,128)} %bitcast.1, bf16[12,6,256,256]{3,2,1,0:T(8,128)(2,1)} %refs_1_.3, bf16[12,6,256,256]{3,2,1,0:T(8,128)(2,1)} %refs_1_.3, ...), custom_call_target="tpu_custom_call" | custom-call | tf_op jit(solution)/shard_map/pallas_call | solution.py:124
  3.9 6.1 %collective-permute-start.3 = (bf16[784,256]{1,0:T(8,128)(2,1)}, bf16[784,256]{1,0:T(8,128)(2,1)S(1)}, u32[]{:S(2)}, u32[]{:S(2)}) collective-permute-start(bf16[784,256]{1,0:T(8,128)(2,1)} %get-tuple-element.16.refs_7_), channel_id=1, source_target_pairs={{0,4},{1,5},{4,2},{5,3},{6,7},{7,6},{8,12},{9,13},{12,10},{13,11},... | collective-permute-start | bytes 1204232 | tf_op jit(solution)/shard_map/ppermute | solution.py:320
  10.0 1.6 %collective-permute-start.2 = (bf16[784,256]{1,0:T(8,128)(2,1)}, bf16[784,256]{1,0:T(8,128)(2,1)S(1)}, u32[]{:S(2)}, u32[]{:S(2)}) collective-permute-start(bf16[784,256]{1,0:T(8,128)(2,1)} %get-tuple-element.16.refs_7_), channel_id=1, source_target_pairs={{4,6},{5,7},{0,1},{1,0},{2,3},{3,2},{6,5},{7,4},{12,14},{13,15},{8... | collective-permute-start | bytes 1204232 | tf_op jit(solution)/shard_map/ppermute | solution.py:320
  11.5 7.3 %collective-permute-done.3.refs_9_ = bf16[784,256]{1,0:T(8,128)(2,1)S(1)} collective-permute-done((bf16[784,256]{1,0:T(8,128)(2,1)}, bf16[784,256]{1,0:T(8,128)(2,1)S(1)}, u32[]{:S(2)}, u32[]{:S(2)}) %collective-permute-start.3) | collective-permute-done | bytes 401440 | tf_op jit(solution)/shard_map/ppermute | solution.py:320
  18.8 2.2 %collective-permute-done.2.refs_11_ = bf16[784,256]{1,0:T(8,128)(2,1)S(1)} collective-permute-done((bf16[784,256]{1,0:T(8,128)(2,1)}, bf16[784,256]{1,0:T(8,128)(2,1)S(1)}, u32[]{:S(2)}, u32[]{:S(2)}) %collective-permute-start.2) | collective-permute-done | bytes 401440 | tf_op jit(solution)/shard_map/ppermute | solution.py:320
  22.0 2.3 %collective-permute-start.5 = (bf16[784,256]{1,0:T(8,128)(2,1)S(1)}, bf16[784,256]{1,0:T(8,128)(2,1)S(1)}, u32[]{:S(2)}, u32[]{:S(2)}) collective-permute-start(bf16[784,256]{1,0:T(8,128)(2,1)S(1)} %select_select_fusion.2), channel_id=1, source_target_pairs={{0,4},{1,5},{4,2},{5,3},{6,7},{7,6},{8,12},{9,13},{12,10},{13,11},... | collective-permute-start | bytes 1204232 | tf_op jit(solution)/shard_map/ppermute | solution.py:320
  24.3 1.6 %collective-permute-start.4 = (bf16[784,256]{1,0:T(8,128)(2,1)S(1)}, bf16[784,256]{1,0:T(8,128)(2,1)S(1)}, u32[]{:S(2)}, u32[]{:S(2)}) collective-permute-start(bf16[784,256]{1,0:T(8,128)(2,1)S(1)} %select_select_fusion.2), channel_id=1, source_target_pairs={{4,6},{5,7},{0,1},{1,0},{2,3},{3,2},{6,5},{7,4},{12,14},{13,15},{8... | collective-permute-start | bytes 1204232 | tf_op jit(solution)/shard_map/ppermute | solution.py:320
  25.9 4.3 %collective-permute-start = (bf16[1584,256]{1,0:T(8,128)(2,1)}, bf16[1584,256]{1,0:T(8,128)(2,1)}, u32[]{:S(2)}, u32[]{:S(2)}) collective-permute-start(bf16[1584,256]{1,0:T(8,128)(2,1)} %get-tuple-element.14), channel_id=1, source_target_pairs={{0,16},{8,24},{1,17},{9,25},{2,18},{10,26},{3,19},{11,27},{4,20},{... | collective-permute-start | bytes 2433032 | tf_op jit(solution)/shard_map/ppermute | solution.py:307
  30.2 1.5 %collective-permute-done.5.refs_8_.refs_16_ = bf16[784,256]{1,0:T(8,128)(2,1)S(1)} collective-permute-done((bf16[784,256]{1,0:T(8,128)(2,1)S(1)}, bf16[784,256]{1,0:T(8,128)(2,1)S(1)}, u32[]{:S(2)}, u32[]{:S(2)}) %collective-permute-start.5) | collective-permute-done | bytes 401440 | tf_op jit(solution)/shard_map/ppermute | solution.py:320
  31.7 2.3 %collective-permute-done.4.refs_10_.refs_18_ = bf16[784,256]{1,0:T(8,128)(2,1)S(1)} collective-permute-done((bf16[784,256]{1,0:T(8,128)(2,1)S(1)}, bf16[784,256]{1,0:T(8,128)(2,1)S(1)}, u32[]{:S(2)}, u32[]{:S(2)}) %collective-permute-start.4) | collective-permute-done | bytes 401440 | tf_op jit(solution)/shard_map/ppermute | solution.py:320
  34.0 1.8 %select_select_fusion.1 = bf16[784,256]{1,0:T(8,128)(2,1)} fusion(bf16[784,256]{1,0:T(8,128)(2,1)} %get-tuple-element.17.refs_21_, bf16[784,256]{1,0:T(8,128)(2,1)S(1)} %collective-permute-done.4.refs_10_.refs_18_, bf16[784,256]{1,0:T(8,128)(2,1)S(1)} %collective-permute-done.5.refs_8_.refs_16_, pred[]{:T(512)S(6)} %eq.36, pred[]{:T(512)S(6)} %eq.37), kind=kLoop, calls=%fused_computation.2 | loop fusion | flops 401408 | bytes 1605634 | tf_op jit(solution)/shard_map/jit(_where)/select_n | solution.py:319
  35.8 1.5 %collective-permute-start.7 = (bf16[784,256]{1,0:T(8,128)(2,1)}, bf16[784,256]{1,0:T(8,128)(2,1)S(1)}, u32[]{:S(2)}, u32[]{:S(2)}) collective-permute-start(bf16[784,256]{1,0:T(8,128)(2,1)} %select_select_fusion.1), channel_id=1, source_target_pairs={{4,6},{5,7},{0,1},{1,0},{2,3},{3,2},{6,5},{7,4},{12,14},{13,15},{8... | collective-permute-start | bytes 1204232 | tf_op jit(solution)/shard_map/ppermute | solution.py:320
  37.3 1.6 %collective-permute-start.6 = (bf16[784,256]{1,0:T(8,128)(2,1)}, bf16[784,256]{1,0:T(8,128)(2,1)S(1)}, u32[]{:S(2)}, u32[]{:S(2)}) collective-permute-start(bf16[784,256]{1,0:T(8,128)(2,1)} %select_select_fusion.1), channel_id=1, source_target_pairs={{0,4},{1,5},{4,2},{5,3},{6,7},{7,6},{8,12},{9,13},{12,10},{13,11},... | collective-permute-start | bytes 1204232 | tf_op jit(solution)/shard_map/ppermute | solution.py:320
  39.0 5.7 %collective-permute-done.7.refs_12_.refs_17_.refs_25_ = bf16[784,256]{1,0:T(8,128)(2,1)S(1)} collective-permute-done((bf16[784,256]{1,0:T(8,128)(2,1)}, bf16[784,256]{1,0:T(8,128)(2,1)S(1)}, u32[]{:S(2)}, u32[]{:S(2)}) %collective-permute-start.7) | collective-permute-done | bytes 401440 | tf_op jit(solution)/shard_map/ppermute | solution.py:320
  46.2 4.2 %collective-permute-start.11 = (bf16[784,256]{1,0:T(8,128)(2,1)S(1)}, bf16[784,256]{1,0:T(8,128)(2,1)S(1)}, u32[]{:S(2)}, u32[]{:S(2)}) collective-permute-start(bf16[784,256]{1,0:T(8,128)(2,1)S(1)} %select_select_fusion), channel_id=1, source_target_pairs={{0,4},{1,5},{4,2},{5,3},{6,7},{7,6},{8,12},{9,13},{12,10},{13,11},... | collective-permute-start | bytes 1204232 | tf_op jit(solution)/shard_map/ppermute | solution.py:320
  50.4 1.5 %collective-permute-start.10 = (bf16[784,256]{1,0:T(8,128)(2,1)S(1)}, bf16[784,256]{1,0:T(8,128)(2,1)S(1)}, u32[]{:S(2)}, u32[]{:S(2)}) collective-permute-start(bf16[784,256]{1,0:T(8,128)(2,1)S(1)} %select_select_fusion), channel_id=1, source_target_pairs={{4,6},{5,7},{0,1},{1,0},{2,3},{3,2},{6,5},{7,4},{12,14},{13,15},{8... | collective-permute-start | bytes 1204232 | tf_op jit(solution)/shard_map/ppermute | solution.py:320
  54.2 3.5 %collective-permute-start.8 = (bf16[256,256]{1,0:T(8,128)(2,1)S(1)}, bf16[256,256]{1,0:T(8,128)(2,1)S(1)}, u32[]{:S(2)}, u32[]{:S(2)}) collective-permute-start(bf16[256,256]{1,0:T(8,128)(2,1)S(1)} %fusion.1), channel_id=1, source_target_pairs={{0,16},{8,24},{1,17},{9,25},{2,18},{10,26},{3,19},{11,27},{4,20},{... | collective-permute-start | bytes 393224 | tf_op jit(solution)/shard_map/ppermute | solution.py:307
  58.4 1.5 %collective-permute-start.13 = (bf16[784,256]{1,0:T(8,128)(2,1)S(1)}, bf16[784,256]{1,0:T(8,128)(2,1)S(1)}, u32[]{:S(2)}, u32[]{:S(2)}) collective-permute-start(bf16[784,256]{1,0:T(8,128)(2,1)S(1)} %broadcast_select_fusion.2), channel_id=1, source_target_pairs={{4,6},{5,7},{0,1},{1,0},{2,3},{3,2},{6,5},{7,4},{12,14},{13,15},{8... | collective-permute-start | bytes 1204232 | tf_op jit(solution)/shard_map/ppermute | solution.py:320
  59.9 2.5 %collective-permute-start.12 = (bf16[784,256]{1,0:T(8,128)(2,1)S(1)}, bf16[784,256]{1,0:T(8,128)(2,1)S(1)}, u32[]{:S(2)}, u32[]{:S(2)}) collective-permute-start(bf16[784,256]{1,0:T(8,128)(2,1)S(1)} %broadcast_select_fusion.2), channel_id=1, source_target_pairs={{0,4},{1,5},{4,2},{5,3},{6,7},{7,6},{8,12},{9,13},{12,10},{13,11},... | collective-permute-start | bytes 1204232 | tf_op jit(solution)/shard_map/ppermute | solution.py:320
  62.6 1.3 %collective-permute-done.9.other_corner = bf16[256,256]{1,0:T(8,128)(2,1)S(1)} collective-permute-done((bf16[256,256]{1,0:T(8,128)(2,1)S(1)}, bf16[256,256]{1,0:T(8,128)(2,1)S(1)}, u32[]{:S(2)}, u32[]{:S(2)}) %collective-permute-start.9) | collective-permute-done | bytes 131104 | tf_op jit(solution)/shard_map/ppermute | solution.py:309
  64.5 4.8 %collective-permute-done.13.refs_26_.refs_10_ = bf16[784,256]{1,0:T(8,128)(2,1)S(1)} collective-permute-done((bf16[784,256]{1,0:T(8,128)(2,1)S(1)}, bf16[784,256]{1,0:T(8,128)(2,1)S(1)}, u32[]{:S(2)}, u32[]{:S(2)}) %collective-permute-start.13) | collective-permute-done | bytes 401440 | tf_op jit(solution)/shard_map/ppermute | solution.py:320
  70.0 5.3 %collective-permute-start.15 = (bf16[784,256]{1,0:T(8,128)(2,1)S(1)}, bf16[784,256]{1,0:T(8,128)(2,1)S(1)}, u32[]{:S(2)}, u32[]{:S(2)}) collective-permute-start(bf16[784,256]{1,0:T(8,128)(2,1)S(1)} %broadcast_select_fusion.1), channel_id=1, source_target_pairs={{0,4},{1,5},{4,2},{5,3},{6,7},{7,6},{8,12},{9,13},{12,10},{13,11},... | collective-permute-start | bytes 1204232 | tf_op jit(solution)/shard_map/ppermute | solution.py:320
  76.0 10.6 %shard_map.61 = (bf16[12,6,256,256]{3,2,1,0:T(8,128)(2,1)}, f32[9,3,256]{2,1,0:T(4,128)S(1)}) custom-call(s32[6,12]{1,0:T(8,128)S(1)} %bitcast.2, bf16[12,6,256,256]{3,2,1,0:T(8,128)(2,1)} %refs_1_.3, f32[12,3,256]{2,1,0:T(4,128)S(1)} %copy-done.8, bf16[512,1536]{1,0:T(8,128)(2,1)S(1)} %get-tuple-element.18.refs_3_, ...), custom_call_target="tpu_custom_call" | custom-call | flops 4831838208 | bytes 18874368 | tf_op jit(solution)/shard_map/pallas_call | solution.py:265
  87.6 6.1 %shard_map.62 = (bf16[12,6,256,256]{3,2,1,0:T(8,128)(2,1)}, f32[3,3,256]{2,1,0:T(4,128)S(1)}) custom-call(s32[6,12]{1,0:T(8,128)S(1)} %bitcast.3, bf16[12,6,256,256]{3,2,1,0:T(8,128)(2,1)} %refs_1_.3, f32[12,3,256]{2,1,0:T(4,128)S(1)} %copy-done.8, bf16[512,1536]{1,0:T(8,128)(2,1)} %copy-done.1, ...), custom_call_target="tpu_custom_call", output_to_operand_aliasing={{0}: (14, {})} | custom-call | flops 1610612736 | bytes 6291456 | tf_op jit(solution)/shard_map/pallas_call | solution.py:265
  (45 shorter events, 9.0 us)
Async XLA Ops:
  3.8 60.1 %copy-start.3 = (bf16[2,256,256]{2,1,0:T(8,128)(2,1)S(1)}, bf16[2,256,256]{2,1,0:T(8,128)(2,1)}, u32[]{:S(2)}) copy-start(bf16[2,256,256]{2,1,0:T(8,128)(2,1)} %refs_6_.3) | copy-start | bytes 786436
  3.8 72.2 %copy-start.5 = (bf16[784,256]{1,0:T(8,128)(2,1)S(1)}, bf16[784,256]{1,0:T(8,128)(2,1)}, u32[]{:S(2)}) copy-start(bf16[784,256]{1,0:T(8,128)(2,1)} %get-tuple-element.15.refs_14_) | copy-start | bytes 1204228
  3.8 72.2 %copy-start.6 = (bf16[784,256]{1,0:T(8,128)(2,1)S(1)}, bf16[784,256]{1,0:T(8,128)(2,1)}, u32[]{:S(2)}) copy-start(bf16[784,256]{1,0:T(8,128)(2,1)} %get-tuple-element.17.refs_21_) | copy-start | bytes 1204228
  3.8 72.2 %copy-start.8 = (f32[12,3,256]{2,1,0:T(4,128)S(1)}, f32[12,3,256]{2,1,0:T(4,128)}, u32[]{:S(2)}) copy-start(f32[12,3,256]{2,1,0:T(4,128)} %refs_2_.3) | copy-start | bytes 110596
  3.8 72.2 %copy-start.9 = (s32[12,6]{0,1:T(8,128)S(1)}, s32[12,6]{0,1:T(8,128)}, u32[]{:S(2)}) copy-start(s32[12,6]{0,1:T(8,128)} %param.5) | copy-start | bytes 868
  3.9 14.9 %collective-permute-start.3 = (bf16[784,256]{1,0:T(8,128)(2,1)}, bf16[784,256]{1,0:T(8,128)(2,1)S(1)}, u32[]{:S(2)}, u32[]{:S(2)}) collective-permute-start(bf16[784,256]{1,0:T(8,128)(2,1)} %get-tuple-element.16.refs_7_), channel_id=1, source_target_pairs={{0,4},{1,5},{4,2},{5,3},{6,7},{7,6},{8,12},{9,13},{12,10},{13,11},... | collective-permute-start | bytes 1204232 | tf_op jit(solution)/shard_map/ppermute | solution.py:320
  10.0 11.0 %collective-permute-start.2 = (bf16[784,256]{1,0:T(8,128)(2,1)}, bf16[784,256]{1,0:T(8,128)(2,1)S(1)}, u32[]{:S(2)}, u32[]{:S(2)}) collective-permute-start(bf16[784,256]{1,0:T(8,128)(2,1)} %get-tuple-element.16.refs_7_), channel_id=1, source_target_pairs={{4,6},{5,7},{0,1},{1,0},{2,3},{3,2},{6,5},{7,4},{12,14},{13,15},{8... | collective-permute-start | bytes 1204232 | tf_op jit(solution)/shard_map/ppermute | solution.py:320
  22.0 9.7 %collective-permute-start.5 = (bf16[784,256]{1,0:T(8,128)(2,1)S(1)}, bf16[784,256]{1,0:T(8,128)(2,1)S(1)}, u32[]{:S(2)}, u32[]{:S(2)}) collective-permute-start(bf16[784,256]{1,0:T(8,128)(2,1)S(1)} %select_select_fusion.2), channel_id=1, source_target_pairs={{0,4},{1,5},{4,2},{5,3},{6,7},{7,6},{8,12},{9,13},{12,10},{13,11},... | collective-permute-start | bytes 1204232 | tf_op jit(solution)/shard_map/ppermute | solution.py:320
  24.3 9.7 %collective-permute-start.4 = (bf16[784,256]{1,0:T(8,128)(2,1)S(1)}, bf16[784,256]{1,0:T(8,128)(2,1)S(1)}, u32[]{:S(2)}, u32[]{:S(2)}) collective-permute-start(bf16[784,256]{1,0:T(8,128)(2,1)S(1)} %select_select_fusion.2), channel_id=1, source_target_pairs={{4,6},{5,7},{0,1},{1,0},{2,3},{3,2},{6,5},{7,4},{12,14},{13,15},{8... | collective-permute-start | bytes 1204232 | tf_op jit(solution)/shard_map/ppermute | solution.py:320
  25.9 26.1 %collective-permute-start = (bf16[1584,256]{1,0:T(8,128)(2,1)}, bf16[1584,256]{1,0:T(8,128)(2,1)}, u32[]{:S(2)}, u32[]{:S(2)}) collective-permute-start(bf16[1584,256]{1,0:T(8,128)(2,1)} %get-tuple-element.14), channel_id=1, source_target_pairs={{0,16},{8,24},{1,17},{9,25},{2,18},{10,26},{3,19},{11,27},{4,20},{... | collective-permute-start | bytes 2433032 | tf_op jit(solution)/shard_map/ppermute | solution.py:307
  35.8 8.9 %collective-permute-start.7 = (bf16[784,256]{1,0:T(8,128)(2,1)}, bf16[784,256]{1,0:T(8,128)(2,1)S(1)}, u32[]{:S(2)}, u32[]{:S(2)}) collective-permute-start(bf16[784,256]{1,0:T(8,128)(2,1)} %select_select_fusion.1), channel_id=1, source_target_pairs={{4,6},{5,7},{0,1},{1,0},{2,3},{3,2},{6,5},{7,4},{12,14},{13,15},{8... | collective-permute-start | bytes 1204232 | tf_op jit(solution)/shard_map/ppermute | solution.py:320
  37.3 7.8 %collective-permute-start.6 = (bf16[784,256]{1,0:T(8,128)(2,1)}, bf16[784,256]{1,0:T(8,128)(2,1)S(1)}, u32[]{:S(2)}, u32[]{:S(2)}) collective-permute-start(bf16[784,256]{1,0:T(8,128)(2,1)} %select_select_fusion.1), channel_id=1, source_target_pairs={{0,4},{1,5},{4,2},{5,3},{6,7},{7,6},{8,12},{9,13},{12,10},{13,11},... | collective-permute-start | bytes 1204232 | tf_op jit(solution)/shard_map/ppermute | solution.py:320
  39.0 37.0 %copy-start.7 = (bf16[784,256]{1,0:T(8,128)(2,1)S(1)}, bf16[784,256]{1,0:T(8,128)(2,1)}, u32[]{:S(2)}) copy-start(bf16[784,256]{1,0:T(8,128)(2,1)} %get-tuple-element.16.refs_7_) | copy-start | bytes 1204228
  46.2 11.5 %collective-permute-start.11 = (bf16[784,256]{1,0:T(8,128)(2,1)S(1)}, bf16[784,256]{1,0:T(8,128)(2,1)S(1)}, u32[]{:S(2)}, u32[]{:S(2)}) collective-permute-start(bf16[784,256]{1,0:T(8,128)(2,1)S(1)} %select_select_fusion), channel_id=1, source_target_pairs={{0,4},{1,5},{4,2},{5,3},{6,7},{7,6},{8,12},{9,13},{12,10},{13,11},... | collective-permute-start | bytes 1204232 | tf_op jit(solution)/shard_map/ppermute | solution.py:320
  50.4 7.9 %collective-permute-start.10 = (bf16[784,256]{1,0:T(8,128)(2,1)S(1)}, bf16[784,256]{1,0:T(8,128)(2,1)S(1)}, u32[]{:S(2)}, u32[]{:S(2)}) collective-permute-start(bf16[784,256]{1,0:T(8,128)(2,1)S(1)} %select_select_fusion), channel_id=1, source_target_pairs={{4,6},{5,7},{0,1},{1,0},{2,3},{3,2},{6,5},{7,4},{12,14},{13,15},{8... | collective-permute-start | bytes 1204232 | tf_op jit(solution)/shard_map/ppermute | solution.py:320
  53.2 10.7 %collective-permute-start.1 = (bf16[1584,256]{1,0:T(8,128)(2,1)S(1)}, bf16[1584,256]{1,0:T(8,128)(2,1)S(1)}, u32[]{:S(2)}, u32[]{:S(2)}) collective-permute-start(bf16[1584,256]{1,0:T(8,128)(2,1)S(1)} %broadcast_select_fusion.mine), channel_id=1, source_target_pairs={{0,8},{8,0},{16,24},{24,16},{1,9},{9,1},{17,25},{25,17},{2,10},{10... | collective-permute-start | bytes 2433032 | tf_op jit(solution)/shard_map/ppermute | solution.py:309
  54.2 8.2 %collective-permute-start.8 = (bf16[256,256]{1,0:T(8,128)(2,1)S(1)}, bf16[256,256]{1,0:T(8,128)(2,1)S(1)}, u32[]{:S(2)}, u32[]{:S(2)}) collective-permute-start(bf16[256,256]{1,0:T(8,128)(2,1)S(1)} %fusion.1), channel_id=1, source_target_pairs={{0,16},{8,24},{1,17},{9,25},{2,18},{10,26},{3,19},{11,27},{4,20},{... | collective-permute-start | bytes 393224 | tf_op jit(solution)/shard_map/ppermute | solution.py:307
  58.3 28.3 %copy-start = (bf16[784,256]{1,0:T(8,128)(2,1)}, bf16[784,256]{1,0:T(8,128)(2,1)S(1)}, u32[]{:S(2)}) copy-start(bf16[784,256]{1,0:T(8,128)(2,1)S(1)} %collective-permute-done.10.refs_19_.refs_24_.refs_11_) | copy-start | bytes 1204228
  58.4 10.9 %collective-permute-start.13 = (bf16[784,256]{1,0:T(8,128)(2,1)S(1)}, bf16[784,256]{1,0:T(8,128)(2,1)S(1)}, u32[]{:S(2)}, u32[]{:S(2)}) collective-permute-start(bf16[784,256]{1,0:T(8,128)(2,1)S(1)} %broadcast_select_fusion.2), channel_id=1, source_target_pairs={{4,6},{5,7},{0,1},{1,0},{2,3},{3,2},{6,5},{7,4},{12,14},{13,15},{8... | collective-permute-start | bytes 1204232 | tf_op jit(solution)/shard_map/ppermute | solution.py:320
  59.9 10.0 %collective-permute-start.12 = (bf16[784,256]{1,0:T(8,128)(2,1)S(1)}, bf16[784,256]{1,0:T(8,128)(2,1)S(1)}, u32[]{:S(2)}, u32[]{:S(2)}) collective-permute-start(bf16[784,256]{1,0:T(8,128)(2,1)S(1)} %broadcast_select_fusion.2), channel_id=1, source_target_pairs={{0,4},{1,5},{4,2},{5,3},{6,7},{7,6},{8,12},{9,13},{12,10},{13,11},... | collective-permute-start | bytes 1204232 | tf_op jit(solution)/shard_map/ppermute | solution.py:320
  62.5 1.4 %collective-permute-start.9 = (bf16[256,256]{1,0:T(8,128)(2,1)S(1)}, bf16[256,256]{1,0:T(8,128)(2,1)S(1)}, u32[]{:S(2)}, u32[]{:S(2)}) collective-permute-start(bf16[256,256]{1,0:T(8,128)(2,1)S(1)} %broadcast_select_fusion.3.corner), channel_id=1, source_target_pairs={{0,8},{8,0},{16,24},{24,16},{1,9},{9,1},{17,25},{25,17},{2,10},{10... | collective-permute-start | bytes 393224 | tf_op jit(solution)/shard_map/ppermute | solution.py:309
  64.5 22.2 %copy-start.1 = (bf16[512,1536]{1,0:T(8,128)(2,1)}, bf16[512,1536]{1,0:T(8,128)(2,1)S(1)}, u32[]{:S(2)}) copy-start(bf16[512,1536]{1,0:T(8,128)(2,1)S(1)} %get-tuple-element.18.refs_3_) | copy-start | bytes 4718596
  70.0 16.7 %collective-permute-start.15 = (bf16[784,256]{1,0:T(8,128)(2,1)S(1)}, bf16[784,256]{1,0:T(8,128)(2,1)S(1)}, u32[]{:S(2)}, u32[]{:S(2)}) collective-permute-start(bf16[784,256]{1,0:T(8,128)(2,1)S(1)} %broadcast_select_fusion.1), channel_id=1, source_target_pairs={{0,4},{1,5},{4,2},{5,3},{6,7},{7,6},{8,12},{9,13},{12,10},{13,11},... | collective-permute-start | bytes 1204232 | tf_op jit(solution)/shard_map/ppermute | solution.py:320
  75.3 11.4 %collective-permute-start.14 = (bf16[784,256]{1,0:T(8,128)(2,1)S(1)}, bf16[784,256]{1,0:T(8,128)(2,1)S(1)}, u32[]{:S(2)}, u32[]{:S(2)}) collective-permute-start(bf16[784,256]{1,0:T(8,128)(2,1)S(1)} %broadcast_select_fusion.1), channel_id=1, source_target_pairs={{4,6},{5,7},{0,1},{1,0},{2,3},{3,2},{6,5},{7,4},{12,14},{13,15},{8... | collective-permute-start | bytes 1204232 | tf_op jit(solution)/shard_map/ppermute | solution.py:320
  (4 other events, 30.6 us)

commit v3 on v2

v3 whole, which is shorter than its diff:
```python
import functools

import jax
import jax.numpy as jnp
from jax import lax
from jax.experimental import pallas as pl
from jax.experimental.pallas import tpu as pltpu
from jax.sharding import PartitionSpec as P

BF = jnp.bfloat16
F32 = jnp.float32
FLAG_ROWS = 16
PIECE_ROWS = 32
MOST_CHUNKS = 3
BATCH = 3
WIDE_VMEM = 54 * 1024 * 1024
VMEM_LIMIT = 20 * 1024 * 1024
UPDATE_VMEM = 44 * 1024 * 1024


def broadcast_plan(groups):
    children = {g: [] for g in range(groups)}

    def hang(low, high, parent):
        if low < high:
            hub = (low + high) // 2
            children[parent].append(hub)
            hang(low, hub, hub)
            hang(hub + 1, high, hub)

    hang(1, groups, 0)
    depth = {0: 0}
    order = [0]
    for g in order:
        for child in children[g]:
            depth[child] = depth[g] + 1
            order.append(child)
    edges = [(g, child, 0) for g in order for child in children[g]]
    spare = {g: 2 - len(children[g]) for g in order}
    orphans = []
    for g in order:
        if spare[g]:
            edges.append((g, g, 1))
            spare[g] -= 1
        else:
            orphans.append(g)
    for g in orphans:
        helper = min((h for h in order if spare[h]), key=lambda h: (depth[h], -h))
        edges.append((helper, g, 1))
        spare[helper] -= 1
    colour = {}
    for start in range(len(edges)):
        if start in colour:
            continue
        colour[start] = 0
        stack = [start]
        while stack:
            e = stack.pop()
            for f in range(len(edges)):
                if f != e and f not in colour and (edges[f][0] == edges[e][0] or edges[f][1] == edges[e][1]):
                    colour[f] = 1 - colour[e]
                    stack.append(f)
    permutes = ([], [])
    own_from, other_from, other_depth = {0: 0}, {}, {}
    for e, (sender, receiver, cross) in enumerate(edges):
        for side in (0, 1):
            permutes[colour[e]].append((2 * sender + side, 2 * receiver + (side ^ cross)))
        if cross:
            other_from[receiver] = colour[e]
            other_depth[receiver] = depth[sender]
        else:
            own_from[receiver] = colour[e]
    return depth, own_from, other_depth, other_from, permutes


def dot(a, b):
    return jnp.dot(a, b, preferred_element_type=F32)


def dot_t(a, b):
    return lax.dot_general(a, b, (((1,), (1,)), ((), ())), preferred_element_type=F32)


def pieces_of(rows):
    n, w = rows.shape
    full = jnp.concatenate([rows, jnp.zeros((8 - n, w), F32)], 0) if n < 8 else rows
    high = full.astype(BF).astype(F32)
    middle = (full - high).astype(BF).astype(F32)
    low = full - high - middle
    return jnp.concatenate([high, middle, low, jnp.zeros((PIECE_ROWS - 24, w), F32)], 0).astype(BF)


def sum_pieces(x, n):
    return (x[0:8] + x[8:16] + x[16:24])[:n]


def slots_of(rows):
    return max(1, rows * 5 // 6)


def chunk_height(rows, width, n):
    return -(-(FLAG_ROWS + slots_of(rows) * width) // (16 * n)) * 16


def pack_kernel(n, height, pattern, column, first_out, later_out, rest_out, packed):
    rows, width = column.shape[0], column.shape[-1]
    slots = slots_of(rows)
    zero = jnp.zeros((), BF)
    lines = lax.broadcasted_iota(jnp.int32, (FLAG_ROWS, width), 0)
    flags = jnp.zeros((FLAG_ROWS, width), F32)
    place = jnp.int32(0)
    for i in range(rows):
        live = pattern[0, i] == 1
        occupied = live | (lax.axis_index("rows") < 2) if i == 0 else live
        start = jnp.where(place < slots, FLAG_ROWS + place * width, n * height + (place - slots) * width)

        @pl.when(occupied)
        def _(i=i, live=live, start=start):
            packed[pl.ds(pl.multiple_of(start, 16), width)] = jnp.where(live, column[i, 0], zero)

        flags = jnp.where((lines == i) & occupied, 1.0, flags)
        place = place + occupied.astype(jnp.int32)
    packed[0:FLAG_ROWS] = flags.astype(BF)
    first_out[...] = packed[0:height]
    for k in range(1, n):
        later_out[k - 1] = packed[k * height : (k + 1) * height]
    rest_out[...] = packed[n * height :]


def pack(blocks, pattern, n, height):
    rows, cols, width, _ = blocks.shape
    rest = (rows - slots_of(rows)) * width
    shapes = [(height, width), (n - 1, height, width), (rest, width)]
    near = pl.BlockSpec(memory_space=pltpu.VMEM)
    return pl.pallas_call(
        functools.partial(pack_kernel, n, height),
        grid=(1,),
        in_specs=[
            pl.BlockSpec(memory_space=pltpu.SMEM),
            pl.BlockSpec((rows, 1, width, width), lambda s: (0, 0, 0, 0)),
        ],
        out_specs=[near] * 3,
        out_shape=[jax.ShapeDtypeStruct(shape, BF) for shape in shapes],
        scratch_shapes=[pltpu.VMEM((n * height + rest, width), BF)],
        compiler_params=pltpu.CompilerParams(vmem_limit_bytes=WIDE_VMEM),
    )(pattern, blocks)


def row_kernel(pattern, row, rhs, out):
    cols, width = row.shape[1], row.shape[-1]
    lines = lax.broadcasted_iota(jnp.int32, (FLAG_ROWS, width), 0)
    flags = jnp.zeros((FLAG_ROWS, width), F32)
    for j in range(cols):
        live = pattern[j, 0] == 1
        out[j * width : (j + 1) * width] = jnp.where(live, row[0, j], jnp.zeros((), BF))
        flags = jnp.where((lines == j) & live, 1.0, flags)
    base = cols * width
    out[base : base + FLAG_ROWS] = flags.astype(BF)
    out[base + FLAG_ROWS : base + FLAG_ROWS + PIECE_ROWS] = pieces_of(rhs[0])


def pack_row(blocks, pattern, right_sides):
    rows, cols, width, _ = blocks.shape
    dirs = right_sides.shape[1]
    shape = (cols * width + FLAG_ROWS + PIECE_ROWS, width)
    return pl.pallas_call(
        row_kernel,
        grid=(1,),
        in_specs=[
            pl.BlockSpec(memory_space=pltpu.SMEM),
            pl.BlockSpec((1, cols, width, width), lambda s: (0, 0, 0, 0)),
            pl.BlockSpec((1, dirs, width), lambda s: (0, 0, 0)),
        ],
        out_specs=pl.BlockSpec(shape, lambda s: (0, 0)),
        out_shape=jax.ShapeDtypeStruct(shape, BF),
        compiler_params=pltpu.CompilerParams(vmem_limit_bytes=WIDE_VMEM),
    )(pattern, blocks, right_sides)


def pick_kernel(tests, places, start, height, *refs):
    sources, out = refs[: len(tests)], refs[-1]
    row_device, col = lax.axis_index("rows"), lax.axis_index("cols")
    for test, place, source in zip(tests, places, sources):

        @pl.when(test(row_device, col))
        def _(place=place, source=source):
            at = slice(start, start + height)
            out[...] = source[at] if place is None else source[place, at]


def pick(choices, start=0, height=None, after=()):
    tests, arrays, places = zip(*((t, *a) if isinstance(a, tuple) else (t, a, None) for t, a in choices))
    height = height or arrays[0].shape[-2]
    after = [a for a in after if all(a is not b for b in arrays)]
    near = pl.BlockSpec(memory_space=pltpu.VMEM)
    return pl.pallas_call(
        functools.partial(pick_kernel, tests, places, start, height),
        in_specs=[near] * len(arrays) + [pl.BlockSpec(memory_space=pl.ANY)] * len(after),
        out_specs=near,
        out_shape=jax.ShapeDtypeStruct((height, arrays[0].shape[-1]), BF),
        compiler_params=pltpu.CompilerParams(vmem_limit_bytes=VMEM_LIMIT),
    )(*arrays, *after)


def corner_kernel(own_tests, cross_tests, slots, *refs):
    sources, out, counts = refs[: len(own_tests) + len(cross_tests)], refs[-2], refs[-1]
    width = out.shape[0] - FLAG_ROWS
    row_device, col = lax.axis_index("rows"), lax.axis_index("cols")
    own_side = (col % 2 == 0) == (row_device % 2 == 1)
    counts[...] = jnp.zeros(counts.shape, F32)
    for k, (test, source) in enumerate(zip(own_tests + cross_tests, sources)):
        wanted = own_side if k < len(own_tests) else jnp.logical_not(own_side)

        @pl.when(test(row_device, col))
        def _(source=source, wanted=wanted):
            taken = jnp.sum(source[0:FLAG_ROWS].astype(F32), 0, keepdims=True)
            counts[...] = jnp.maximum(counts[...], taken)

            @pl.when(wanted)
            def _():
                out[0:width] = source[FLAG_ROWS : FLAG_ROWS + width]

    out[width:] = jnp.where(counts[0:FLAG_ROWS] > slots, 1.0, 0.0).astype(BF)


def corner_of(own, cross, slots, width):
    near = pl.BlockSpec(memory_space=pltpu.VMEM)
    own_tests, cross_tests = [t for t, _ in own], [t for t, _ in cross]
    return pl.pallas_call(
        functools.partial(corner_kernel, own_tests, cross_tests, slots),
        in_specs=[near] * len(own + cross),
        out_specs=near,
        out_shape=jax.ShapeDtypeStruct((width + FLAG_ROWS, width), BF),
        scratch_shapes=[pltpu.VMEM((FLAG_ROWS, width), F32)],
        compiler_params=pltpu.CompilerParams(vmem_limit_bytes=VMEM_LIMIT),
    )(*[a for _, a in own + cross])


def merge_kernel(bound, mine, moved, out):
    width = out.shape[0] - FLAG_ROWS
    keep = lax.axis_index("rows") < bound
    out[0:width] = jnp.where(keep, mine[0:width], moved[0:width])
    out[width:] = jnp.maximum(mine[width:].astype(F32), moved[width:].astype(F32)).astype(BF)


def merge(bound, mine, moved):
    near = pl.BlockSpec(memory_space=pltpu.VMEM)
    return pl.pallas_call(
        functools.partial(merge_kernel, bound),
        in_specs=[near] * 2,
        out_specs=near,
        out_shape=jax.ShapeDtypeStruct(mine.shape, BF),
        compiler_params=pltpu.CompilerParams(vmem_limit_bytes=VMEM_LIMIT),
    )(mine, moved)


def panel_kernel(dirs, ncols, mine, other, corner, other_corner, inverse, upper, upper_one, sides, over):
    width = inverse.shape[-1]
    cols = upper.shape[1] // width
    even = lax.axis_index("rows") % 2 == 0
    col = lax.axis_index("cols")

    def pick(lo, hi):
        a, b = mine[lo:hi], other[lo:hi]
        return jnp.where(even, a, b), jnp.where(even, b, a)

    zero = jnp.zeros((), BF)
    over[...] = jnp.maximum(corner[width:].astype(F32), other_corner[width:].astype(F32))[:, 0:128]
    upper_one[...] = jnp.where(even, corner[0:width], other_corner[0:width])
    lower_one = dot(jnp.where(even, other_corner[0:width], corner[0:width]), inverse[0]).astype(BF)
    base = cols * width
    flags = pick(base, base + FLAG_ROWS)[1].astype(F32)
    for j in range(cols):
        zeroth, first = pick(j * width, (j + 1) * width)
        zeroth = jnp.where(j * ncols + col > 0, zeroth, zero)
        fresh = (first.astype(F32) - dot(lower_one, zeroth)).astype(BF)
        keep = (flags[j : j + 1] > 0.5) & (j * ncols + col > 1)
        at = slice(j * width, (j + 1) * width)
        upper[0:width, at] = zeroth
        upper[width : 2 * width, at] = jnp.where(keep, fresh, zero)
    side_zero, side_one = pick(base + FLAG_ROWS, base + FLAG_ROWS + PIECE_ROWS)
    sides[0] = side_zero
    later = sum_pieces(side_one.astype(F32), dirs) - sum_pieces(dot_t(side_zero, lower_one), dirs)
    sides[1] = pieces_of(later)


def panel(dirs, cols, ncols, mine, other, corner, other_corner, inverse):
    width = inverse.shape[-1]
    return pl.pallas_call(
        functools.partial(panel_kernel, dirs, ncols),
        out_shape=[
            jax.ShapeDtypeStruct((2 * width, cols * width), BF),
            jax.ShapeDtypeStruct((width, width), BF),
            jax.ShapeDtypeStruct((2, PIECE_ROWS, width), BF),
            jax.ShapeDtypeStruct((FLAG_ROWS, 128), F32),
        ],
        compiler_params=pltpu.CompilerParams(vmem_limit_bytes=VMEM_LIMIT),
        cost_estimate=pl.CostEstimate(
            flops=2 * (cols + 2) * width**3, bytes_accessed=8 * cols * width**2, transcendentals=0
        ),
    )(mine, other, corner, other_corner, inverse)


def update_kernel(n, height, nrows, ncols, sources, n_refs, last, *refs):
    pattern, blocks = refs[:2]
    given, landed, extra = refs[2:7], refs[7 : 7 + n_refs], refs[7 + n_refs : 10 + n_refs]
    outs = refs[7 + n_refs + (4 if last else 1) :]
    out, forward = outs[:2]
    scratch = outs[2 if last else 3 :]
    columns, lower, work, flags_v, flags_s, slot_of, order, in_sems, out_sems, flag_sem = scratch[:10]
    row_device, col = lax.axis_index("rows"), lax.axis_index("cols")
    pair, side = col // 2, col % 2
    zero = jnp.zeros((), BF)
    rows, cols, width = work.shape[:3]
    slots = slots_of(rows)

    copies = []
    if last:
        near, given_sems, column_sems = scratch[10:15], scratch[15], scratch[16]
        rest_own, rest_cross, done = extra
        tail = slice(n * height, None)
        moves = list(zip(given, near)) + [(done, forward)]
        moves += [(rest_own, columns.at[side, tail]), (rest_cross, columns.at[1 - side, tail])]
        for m, (source, target) in enumerate(moves):
            copies.append(pltpu.make_async_copy(source, target, given_sems.at[m]))
            copies[-1].start()
    else:
        near = given
        outs[2][...] = extra[0][...]
    rhs, upper, upper_one, sides, inverse = near

    for k, per_chunk in enumerate(sources):
        for which in (0, 1):
            for ref, pairs in per_chunk[which]:
                hit = functools.reduce(jnp.logical_or, [pair == g for g in pairs])

                @pl.when(hit)
                def _(source=landed[ref[0]], place=ref[1], which=which, k=k):
                    source = source if place is None else source.at[place]
                    at = slice(k * height, (k + 1) * height)
                    target = columns.at[side if which == 0 else 1 - side, at]
                    if last:
                        pltpu.make_async_copy(source, target, column_sems.at[k, which]).start()
                    else:
                        target[...] = source[...]

    if last:
        for copy in copies:
            copy.wait()
        for k in range(n):
            for which in (0, 1):
                at = slice(k * height, (k + 1) * height)
                target = columns.at[side if which == 0 else 1 - side, at]
                pltpu.make_async_copy(target, target, column_sems.at[k, which]).wait()

    for b in (0, 1):
        flags_v[b * FLAG_ROWS : (b + 1) * FLAG_ROWS] = columns[b, 0:FLAG_ROWS].astype(F32)[:, 0:128].astype(jnp.int32)
    copy = pltpu.make_async_copy(flags_v, flags_s, flag_sem)
    copy.start()
    copy.wait()

    early = ((n - 1) * height - FLAG_ROWS) // width
    zeroth = first = count = jnp.int32(0)
    for i in range(rows):
        occupied = flags_s[i, 0], flags_s[FLAG_ROWS + i, 0]
        slot_zeroth, slot_first = jnp.where(occupied[0] > 0, zeroth, -1), jnp.where(occupied[1] > 0, first, -1)
        slot_of[0, i] = slot_zeroth
        slot_of[1, i] = slot_first
        ready = (slot_zeroth < early) & (slot_first < early)
        mine = jnp.logical_not(ready) if last else ready
        order[count] = i
        count = count + mine.astype(jnp.int32)
        zeroth, first = zeroth + occupied[0], first + occupied[1]

    def row_at(t):
        return order[jnp.minimum(t, count - 1)]

    def fetch(t):
        return pltpu.make_async_copy(blocks.at[row_at(t)], work.at[t], in_sems.at[t])

    def send(t):
        return pltpu.make_async_copy(work.at[t], out.at[row_at(t)], out_sems.at[t])

    @pl.loop(0, count)
    def _(t):
        fetch(t).start()

    if not last:
        forward[...] = rhs[...]

    def block_at(b, i):
        slot = slot_of[b, i]
        start = jnp.where(slot < slots, FLAG_ROWS + slot * width, n * height + (slot - slots) * width)
        start = jnp.where(slot < 0, 0, start)
        return jnp.where(slot >= 0, columns[b, pl.ds(pl.multiple_of(start, 16), width)], zero)

    @pl.loop(0, (count + BATCH - 1) // BATCH)
    def _(g):
        members = [row_at(g * BATCH + t) for t in range(BATCH)]
        globs = [i * nrows + row_device for i in members]
        parts = [slice(t * width, (t + 1) * width) for t in range(BATCH)]
        product = dot(jnp.concatenate([block_at(0, i) for i in members], 0), inverse[0])
        lower_zero = jnp.concatenate(
            [jnp.where(glob > 0, product[at], 0.0).astype(BF) for glob, at in zip(globs, parts)], 0
        )
        change = dot(lower_zero, upper_one[...])
        pivots = []
        for i, at in zip(members, parts):
            fresh = (block_at(1, i).astype(F32) - change[at]).astype(BF)
            pivots.append(jnp.where(slot_of[1, i] >= 0, fresh, zero))
        product = dot(jnp.concatenate(pivots, 0), inverse[1])
        for t, (glob, at) in enumerate(zip(globs, parts)):
            lower[g * BATCH + t, :, 0:width] = lower_zero[at]
            lower[g * BATCH + t, :, width : 2 * width] = jnp.where(glob > 1, product[at], 0.0).astype(BF)

    @pl.loop(0, count)
    def _(t):
        i = row_at(t)
        glob = i * nrows + row_device
        dirs = rhs.shape[1]
        fetch(t).wait()
        head = rhs[i] - sum_pieces(dot_t(sides[0], lower[t, :, 0:width]), dirs)
        forward[i] = head - sum_pieces(dot_t(sides[1], lower[t, :, width : 2 * width]), dirs)
        lower_zeroth = (col == 0) & (glob > 0)
        lower_first = (col == 1) & (glob > 1)
        for j in range(cols):
            change = dot(lower[t], upper[:, j * width : (j + 1) * width])
            fresh = (work[t, j].astype(F32) - change).astype(BF)
            fresh = jnp.where(pattern[j, i] == 1, fresh, zero)
            if j == 0:
                fresh = jnp.where(lower_zeroth, lower[t, :, 0:width], fresh)
                fresh = jnp.where(lower_first, lower[t, :, width : 2 * width], fresh)
            work[t, j] = fresh
        send(t).start()

    @pl.loop(0, count)
    def _(t):
        send(t).wait()


def update(n, height, nrows, ncols, sources, landed, pattern, blocks, given, extra, last):
    rows, cols, width, _ = blocks.shape
    far = pl.BlockSpec(memory_space=pl.ANY)
    near = pl.BlockSpec(memory_space=pltpu.VMEM)
    rest = (rows - slots_of(rows)) * width
    most = -(-rows // BATCH) * BATCH
    rhs = given[0]
    out_shape = [jax.ShapeDtypeStruct(blocks.shape, BF), jax.ShapeDtypeStruct(rhs.shape, F32)]
    scratch = [
        pltpu.VMEM((2, n * height + rest, width), BF),
        pltpu.VMEM((most, width, 2 * width), BF),
        pltpu.VMEM((rows, cols, width, width), BF),
        pltpu.VMEM((2 * FLAG_ROWS, 128), jnp.int32),
        pltpu.SMEM((2 * FLAG_ROWS, 128), jnp.int32),
        pltpu.SMEM((2, rows), jnp.int32),
        pltpu.SMEM((rows + 1,), jnp.int32),
        pltpu.SemaphoreType.DMA((rows,)),
        pltpu.SemaphoreType.DMA((rows,)),
        pltpu.SemaphoreType.DMA,
    ]
    if last:
        scratch += [pltpu.VMEM(a.shape, a.dtype) for a in given]
        scratch += [pltpu.SemaphoreType.DMA((len(given) + 3,)), pltpu.SemaphoreType.DMA((n, 2))]
    else:
        out_shape.append(jax.ShapeDtypeStruct(extra[0].shape, F32))
    place = far if last else near
    arrays = (*given, *landed, *extra)
    return pl.pallas_call(
        functools.partial(update_kernel, n, height, nrows, ncols, sources, len(landed), last),
        in_specs=[pl.BlockSpec(memory_space=pltpu.SMEM), far] + [place] * len(arrays),
        out_specs=[far] + [near] * (len(out_shape) - 1),
        out_shape=out_shape,
        scratch_shapes=scratch,
        input_output_aliases={1 + len(arrays): 0} if last else {},
        compiler_params=pltpu.CompilerParams(vmem_limit_bytes=WIDE_VMEM if last else UPDATE_VMEM),
        cost_estimate=pl.CostEstimate(
            flops=2 * rows * (cols + 2) * width**3, bytes_accessed=2 * rows * (cols + 2) * width**2, transcendentals=0
        ),
    )(pattern, blocks, *arrays)


def on_device(blocks, pattern, pivot_inverse, right_sides):
    rows, cols, width, _ = blocks.shape
    dirs = right_sides.shape[1]
    nrows = lax.axis_size("rows")
    ncols = lax.axis_size("cols")
    groups = ncols // 2
    depth, own_from, other_depth, other_from, permutes = broadcast_plan(groups)
    n = max(d for d in range(2, MOST_CHUNKS + 1))
    height = chunk_height(rows, width, n)
    slots = slots_of(rows)
    pattern = pattern.T
    start, later, rest = pack(blocks, pattern, n, height)
    columns = [start] + [(later, k) for k in range(n - 1)]
    row = pack_row(blocks, pattern, right_sides)

    def among(members):
        return lambda row_device, col: functools.reduce(jnp.logical_or, [col // 2 == g for g in members])

    def down_rows(x):
        reach = 1
        while reach < nrows // 2:
            hops = [(2 * h + s, 2 * (h + reach) + s) for h in range(min(reach, nrows // 2 - reach)) for s in (0, 1)]
            moved = lax.ppermute(x, "rows", hops)
            bound = 2 * reach
            x = pick([(lambda r, c, b=bound: r < b, x), (lambda r, c, b=bound: r >= b, moved)])
            reach *= 2
        return x, lax.ppermute(x, "rows", [(r, r ^ 1) for r in range(nrows)])

    def across_rows(x):
        pairs, reach = nrows // 2, 1
        if pairs & (pairs - 1):
            flags = lax.pmax(x[width:].astype(F32), "rows").astype(BF)
            x = jnp.concatenate([x[:width], flags], 0)
            return down_rows(x)
        while reach < pairs:
            x = merge(2 * reach, x, lax.ppermute(x, "rows", [(r, r ^ (2 * reach)) for r in range(nrows)]))
            reach *= 2
        return x, lax.ppermute(x, "rows", [(r, r ^ 1) for r in range(nrows)])

    def places(k):
        own, cross = {}, {}
        for g in range(groups):
            key = ("here", k) if g == 0 else (own_from[g], k + depth[g] - 1)
            own.setdefault(key, []).append(g)
            cross.setdefault((other_from[g], k + other_depth[g]), []).append(g)
        return own, cross

    def array_at(key, columns, landed):
        return columns[key[1]] if key[0] == "here" else landed[key[1]][key[0]]

    def travel(columns, landed, step, after=()):
        count = len(columns)
        active = [g for g in range(groups) if 0 <= step - depth[g] < count]
        choices = []
        if 0 in active:
            choices.append((among([0]), columns[step]))
        for which in (0, 1):
            members = [g for g in active if g and own_from[g] == which]
            if members:
                choices.append((among(members), landed[step - 1][which]))
        payload = columns[0]
        if step:
            payload = pick(choices, after=[a for a in landed[-1] if a is not None] + list(after))
        pairs = [[p for p in permutes[which] if p[0] // 2 in active] for which in (0, 1)]
        return [lax.ppermute(payload, "cols", p) if p else None for p in pairs]

    deepest = max(other_depth.values())
    lag = max(max(depth.values()) - 1, deepest) + 1

    def corners():
        own, cross = ([(among(m), array_at(k, columns, landed)) for k, m in found.items()] for found in places(0))
        return across_rows(corner_of(own, cross, slots, width))

    def update_with(chunks, extra, last):
        arrays, sources = [], []
        for k in range(chunks):
            sources.append([])
            for which in places(k):
                found = []
                for key, members in which.items():
                    array, place = array_at(key, columns, landed), None
                    if isinstance(array, tuple):
                        array, place = array
                    found.append(((len(arrays), place), members))
                    arrays.append(array)
                sources[-1].append(found)
        given = (right_sides, upper, upper_one, sides, pivot_inverse)
        return update(n, height, nrows, ncols, sources, arrays, pattern, blocks, given, extra, last)

    mine, other = down_rows(row)
    landed = []
    for step in range(n + deepest):
        after = []
        if step == lag + 1:
            corner, other_corner = corners()
            after.append(corner)
        landed.append(travel(columns, landed, step, after))
    if n + deepest <= lag + 1:
        corner, other_corner = corners()
    upper, upper_one, sides, over = panel(dirs, cols, ncols, mine, other, corner, other_corner, pivot_inverse)
    out, forward, over = update_with(n - 1, (over,), False)

    def fetch_rest(rest):
        got = []
        for step in range(1 + deepest):
            got.append(travel([rest], got, step))
        own, cross = places(0)
        return tuple(pick([(among(m), array_at(k, [rest], got)) for k, m in found.items()]) for found in (own, cross))

    rest_own, rest_cross = lax.cond(over[0, 0] > 0.5, fetch_rest, lambda rest: (rest, rest), rest)
    return tuple(update_with(n, (rest_own, rest_cross, forward, out), True))


def solution(mesh):
    return jax.shard_map(
        on_device,
        mesh=mesh,
        in_specs=(P("rows", "cols", None, None), P("rows", "cols"), P(), P("rows", None, None)),
        out_specs=(P("rows", "cols", None, None), P("rows", None, None)),
        check_vma=False,
    )
```

time: 94.8 us -> 88.5 us (0.934)
  the two profiles are of different devices: /device:TPU:0 before, /device:TPU:24 now
where the time goes in v3:
time: 88.5 us; the launch traced here: 88 us
  waiting for transfers between devices  29.8 us (34%)
  starting transfers between devices  27.9 us (32%)
  Pallas kernels  25.9 us (29%)
  local copies, waits for them, and re-layouts  2.67 us (3%)
  between operations  1.72 us (2%)
    ppermute x10, waiting for transfers between devices, travel(): return [lax.ppermute(payload, 'cols', p) if p else None for p in pairs]  26.2 us
    ppermute x10, starting transfers between devices, travel(): return [lax.ppermute(payload, 'cols', p) if p else None for p in pairs]  22.5 us
    pallas_call x2, Pallas kernels, update(): pl.pallas_call(functools.partial(update_kernel, n, height, nrows, ncols,...  20.3 us
    ppermute x1, starting transfers between devices, down_rows(): moved = lax.ppermute(x, 'rows', hops)  3.59 us
    ppermute x1, waiting for transfers between devices, across_rows(): lax.ppermute(x, 'rows', [(r, r ^ 2 * reach) for r in range(nrows)])  3.51 us
    pallas_call x1, Pallas kernels, pack(): pl.pallas_call(functools.partial(pack_kernel, n, height), grid=(1,), in_s...  2.68 us
    unnamed x40, local copies, waits for them, and re-layouts  2.14 us
    pallas_call x1, Pallas kernels, pack_row(): pl.pallas_call(row_kernel, grid=(1,), in_specs=[pl.BlockSpec(memory_space...  2.09 us
  transfers between devices with their start and end apart: 14, of which 5 were waited for; matrix products, arithmetic and copies ran while one was open for 1% of the time, Pallas kernels for 18%

profile of v3, /device:TPU:24, one launch (start us, length us, event | category | flops | bytes accessed | tf_op | source)
XLA Modules:
  0.0 88.0 jit_solution(6230918853641328652)
XLA Ops:
  0.6 2.7 %shard_map.61 = (bf16[864,256]{1,0:T(8,128)(2,1)}, bf16[2,864,256]{2,1,0:T(8,128)(2,1)}, bf16[512,256]{1,0:T(8,128)(2,1)S(1)}) custom-call(s32[6,12]{1,0:T(8,128)} %bitcast.2, bf16[12,6,256,256]{3,2,1,0:T(8,128)(2,1)} %refs_1_.3), custom_call_target="tpu_custom_call" | custom-call | tf_op jit(solution)/shard_map/pallas_call | solution.py:135
  3.3 0.8 collective-permute-start.9
  4.1 0.7 collective-permute-start.8
  4.8 2.1 %shard_map.59.refs_0_ = bf16[1584,256]{1,0:T(8,128)(2,1)} custom-call(s32[6,12]{1,0:T(8,128)} %bitcast.3, bf16[12,6,256,256]{3,2,1,0:T(8,128)(2,1)} %refs_1_.3, f32[12,3,256]{2,1,0:T(4,128)} %refs_2_.3), custom_call_target="tpu_custom_call" | custom-call | tf_op jit(solution)/shard_map/pallas_call | solution.py:166
  6.9 3.6 %collective-permute-start.6 = (bf16[1584,256]{1,0:T(8,128)(2,1)}, bf16[1584,256]{1,0:T(8,128)(2,1)S(1)}, u32[]{:S(2)}, u32[]{:S(2)}) collective-permute-start(bf16[1584,256]{1,0:T(8,128)(2,1)} %shard_map.59.refs_0_), channel_id=1, source_target_pairs={{0,16},{8,24},{1,17},{9,25},{2,18},{10,26},{3,19},{11,27},{4,20},{... | collective-permute-start | bytes 2433032 | tf_op jit(solution)/shard_map/ppermute | solution.py:504
  10.6 1.3 %collective-permute-start.11 = (bf16[864,256]{1,0:T(8,128)(2,1)S(1)}, bf16[864,256]{1,0:T(8,128)(2,1)S(1)}, u32[]{:S(2)}, u32[]{:S(2)}) collective-permute-start(bf16[864,256]{1,0:T(8,128)(2,1)S(1)} %shard_map.62), channel_id=1, source_target_pairs={{4,6},{5,7},{0,1},{1,0},{12,14},{13,15},{8,9},{9,8},{20,22},{21,23... | collective-permute-start | bytes 1327112 | tf_op jit(solution)/shard_map/ppermute | solution.py:546
  11.9 0.7 collective-permute-start.10
  12.6 17.5 %collective-permute-done.11.refs_2_.refs_3_.refs_10_.refs_18_ = bf16[864,256]{1,0:T(8,128)(2,1)S(1)} collective-permute-done((bf16[864,256]{1,0:T(8,128)(2,1)S(1)}, bf16[864,256]{1,0:T(8,128)(2,1)S(1)}, u32[]{:S(2)}, u32[]{:S(2)}) %collective-permute-start.11) | collective-permute-done | bytes 442400 | tf_op jit(solution)/shard_map/ppermute | solution.py:546
  30.2 3.4 %collective-permute-start.13 = (bf16[864,256]{1,0:T(8,128)(2,1)S(1)}, bf16[864,256]{1,0:T(8,128)(2,1)S(1)}, u32[]{:S(2)}, u32[]{:S(2)}) collective-permute-start(bf16[864,256]{1,0:T(8,128)(2,1)S(1)} %shard_map.63), channel_id=1, source_target_pairs={{0,4},{1,5},{4,2},{5,3},{6,7},{7,6},{8,12},{9,13},{12,10},{13,11},... | collective-permute-start | bytes 1327112 | tf_op jit(solution)/shard_map/ppermute | solution.py:546
  33.6 4.1 %collective-permute-start.12 = (bf16[864,256]{1,0:T(8,128)(2,1)S(1)}, bf16[864,256]{1,0:T(8,128)(2,1)S(1)}, u32[]{:S(2)}, u32[]{:S(2)}) collective-permute-start(bf16[864,256]{1,0:T(8,128)(2,1)S(1)} %shard_map.63), channel_id=1, source_target_pairs={{4,6},{5,7},{0,1},{1,0},{2,3},{3,2},{6,5},{7,4},{12,14},{13,15},{8... | collective-permute-start | bytes 1327112 | tf_op jit(solution)/shard_map/ppermute | solution.py:546
  37.7 1.1 %copy-done.11 = bf16[1584,256]{1,0:T(8,128)(2,1)S(1)} copy-done((bf16[1584,256]{1,0:T(8,128)(2,1)S(1)}, bf16[1584,256]{1,0:T(8,128)(2,1)}, u32[]{:S(2)}) %copy-start.11) | copy-done | bytes 811032
  39.0 3.5 %collective-permute-done.13.refs_6_.refs_0_.refs_13_.refs_15_.refs_23_ = bf16[864,256]{1,0:T(8,128)(2,1)S(1)} collective-permute-done((bf16[864,256]{1,0:T(8,128)(2,1)S(1)}, bf16[864,256]{1,0:T(8,128)(2,1)S(1)}, u32[]{:S(2)}, u32[]{:S(2)}) %collective-permute-start.13) | collective-permute-done | bytes 442400 | tf_op jit(solution)/shard_map/ppermute | solution.py:546
  42.5 2.8 %collective-permute-done.12.refs_5_.refs_1_.refs_12_.refs_17_.refs_25_ = bf16[864,256]{1,0:T(8,128)(2,1)S(1)} collective-permute-done((bf16[864,256]{1,0:T(8,128)(2,1)S(1)}, bf16[864,256]{1,0:T(8,128)(2,1)S(1)}, u32[]{:S(2)}, u32[]{:S(2)}) %collective-permute-start.12) | collective-permute-done | bytes 442400 | tf_op jit(solution)/shard_map/ppermute | solution.py:546
  45.4 3.2 %collective-permute-start.17 = (bf16[864,256]{1,0:T(8,128)(2,1)S(1)}, bf16[864,256]{1,0:T(8,128)(2,1)S(1)}, u32[]{:S(2)}, u32[]{:S(2)}) collective-permute-start(bf16[864,256]{1,0:T(8,128)(2,1)S(1)} %shard_map.67), channel_id=1, source_target_pairs={{4,2},{5,3},{6,7},{7,6},{12,10},{13,11},{14,15},{15,14},{20,18},{2... | collective-permute-start | bytes 1327112 | tf_op jit(solution)/shard_map/ppermute | solution.py:546
  48.6 3.4 %collective-permute-start.16 = (bf16[864,256]{1,0:T(8,128)(2,1)S(1)}, bf16[864,256]{1,0:T(8,128)(2,1)S(1)}, u32[]{:S(2)}, u32[]{:S(2)}) collective-permute-start(bf16[864,256]{1,0:T(8,128)(2,1)S(1)} %shard_map.67), channel_id=1, source_target_pairs={{4,6},{5,7},{2,3},{3,2},{6,5},{7,4},{12,14},{13,15},{10,11},{11,10... | collective-permute-start | bytes 1327112 | tf_op jit(solution)/shard_map/ppermute | solution.py:546
  52.1 1.6 %collective-permute-start.14 = (bf16[272,256]{1,0:T(8,128)(2,1)S(1)}, bf16[272,256]{1,0:T(8,128)(2,1)S(1)}, u32[]{:S(2)}, u32[]{:S(2)}) collective-permute-start(bf16[272,256]{1,0:T(8,128)(2,1)S(1)} %shard_map.64.mine), channel_id=1, source_target_pairs={{0,16},{8,24},{16,0},{24,8},{1,17},{9,25},{17,1},{25,9},{2,18},{10... | collective-permute-start | bytes 417800 | tf_op jit(solution)/shard_map/ppermute | solution.py:517
  53.7 3.5 %collective-permute-done.14.moved = bf16[272,256]{1,0:T(8,128)(2,1)S(1)} collective-permute-done((bf16[272,256]{1,0:T(8,128)(2,1)S(1)}, bf16[272,256]{1,0:T(8,128)(2,1)S(1)}, u32[]{:S(2)}, u32[]{:S(2)}) %collective-permute-start.14) | collective-permute-done | bytes 139296 | tf_op jit(solution)/shard_map/ppermute | solution.py:517
  57.3 2.3 %collective-permute-done.16.refs_1_.refs_19_.refs_24_ = bf16[864,256]{1,0:T(8,128)(2,1)S(1)} collective-permute-done((bf16[864,256]{1,0:T(8,128)(2,1)S(1)}, bf16[864,256]{1,0:T(8,128)(2,1)S(1)}, u32[]{:S(2)}, u32[]{:S(2)}) %collective-permute-start.16) | collective-permute-done | bytes 442400 | tf_op jit(solution)/shard_map/ppermute | solution.py:546
  59.7 2.5 %collective-permute-start.19 = (bf16[864,256]{1,0:T(8,128)(2,1)S(1)}, bf16[864,256]{1,0:T(8,128)(2,1)S(1)}, u32[]{:S(2)}, u32[]{:S(2)}) collective-permute-start(bf16[864,256]{1,0:T(8,128)(2,1)S(1)} %shard_map.68), channel_id=1, source_target_pairs={{6,7},{7,6},{14,15},{15,14},{22,23},{23,22},{30,31},{31,30}} | collective-permute-start | bytes 1327112 | tf_op jit(solution)/shard_map/ppermute | solution.py:546
  62.2 2.5 %collective-permute-start.18 = (bf16[864,256]{1,0:T(8,128)(2,1)S(1)}, bf16[864,256]{1,0:T(8,128)(2,1)S(1)}, u32[]{:S(2)}, u32[]{:S(2)}) collective-permute-start(bf16[864,256]{1,0:T(8,128)(2,1)S(1)} %shard_map.68), channel_id=1, source_target_pairs={{2,3},{3,2},{6,5},{7,4},{10,11},{11,10},{14,13},{15,12},{18,19},{1... | collective-permute-start | bytes 1327112 | tf_op jit(solution)/shard_map/ppermute | solution.py:546
  64.7 0.5 shard_map.66
  65.3 12.8 %shard_map.69 = (bf16[12,6,256,256]{3,2,1,0:T(8,128)(2,1)}, f32[12,3,256]{2,1,0:T(4,128)S(1)}, f32[16,128]{1,0:T(8,128)S(1)}) custom-call(s32[6,12]{1,0:T(8,128)S(1)} %bitcast.5, bf16[12,6,256,256]{3,2,1,0:T(8,128)(2,1)} %refs_1_.3, f32[12,3,256]{2,1,0:T(4,128)S(1)} %copy-done.14, bf16[512,1536]{1,0:T(8,128)(2,1)S(1)} %get-tuple-element.18.refs_3_, ...), custom_call_target="tpu_custom_call" | custom-call | flops 3221225472 | bytes 12582912 | tf_op jit(solution)/shard_map/pallas_call | solution.py:468
  79.5 0.7 copy-done.18
  80.4 7.6 %shard_map.70 = (bf16[12,6,256,256]{3,2,1,0:T(8,128)(2,1)}, f32[12,3,256]{2,1,0:T(4,128)}) custom-call(s32[6,12]{1,0:T(8,128)} %bitcast.4, bf16[12,6,256,256]{3,2,1,0:T(8,128)(2,1)} %refs_1_.3, f32[12,3,256]{2,1,0:T(4,128)} %refs_2_.3, bf16[512,1536]{1,0:T(8,128)(2,1)} %copy-done.9, bf16[256,256]{1,0:T(8,128)(2,1)} %copy-done.13, ...), custom_call_target="tpu_custom_call", output_to_operand_aliasing={{0}: (31, {})} | custom-call | flops 3221225472 | bytes 12582912 | tf_op jit(solution)/shard_map/pallas_call | solution.py:468
  (59 shorter events, 1.3 us)
Async XLA Ops:
  3.3 48.7 %copy-start.10 = (bf16[864,256]{1,0:T(8,128)(2,1)S(1)}, bf16[864,256]{1,0:T(8,128)(2,1)}, u32[]{:S(2)}) copy-start(bf16[864,256]{1,0:T(8,128)(2,1)} %get-tuple-element.16.refs_0_.refs_7_) | copy-start | bytes 1327108
  3.3 61.4 %copy-start.12 = (bf16[2,256,256]{2,1,0:T(8,128)(2,1)S(1)}, bf16[2,256,256]{2,1,0:T(8,128)(2,1)}, u32[]{:S(2)}) copy-start(bf16[2,256,256]{2,1,0:T(8,128)(2,1)} %refs_6_.3) | copy-start | bytes 786436
  3.3 7.2 %collective-permute-start.9 = (bf16[864,256]{1,0:T(8,128)(2,1)}, bf16[864,256]{1,0:T(8,128)(2,1)S(1)}, u32[]{:S(2)}, u32[]{:S(2)}) collective-permute-start(bf16[864,256]{1,0:T(8,128)(2,1)} %get-tuple-element.16.refs_0_.refs_7_), channel_id=1, source_target_pairs={{0,1},{1,0},{8,9},{9,8},{16,17},{17,16},{24,25},{25,24}} | collective-permute-start | bytes 1327112 | tf_op jit(solution)/shard_map/ppermute | solution.py:546
  4.1 6.4 %collective-permute-start.8 = (bf16[864,256]{1,0:T(8,128)(2,1)}, bf16[864,256]{1,0:T(8,128)(2,1)S(1)}, u32[]{:S(2)}, u32[]{:S(2)}) collective-permute-start(bf16[864,256]{1,0:T(8,128)(2,1)} %get-tuple-element.16.refs_0_.refs_7_), channel_id=1, source_target_pairs={{0,4},{1,5},{8,12},{9,13},{16,20},{17,21},{24,28},{25,29}} | collective-permute-start | bytes 1327112 | tf_op jit(solution)/shard_map/ppermute | solution.py:546
  6.9 58.4 %copy-start.14 = (f32[12,3,256]{2,1,0:T(4,128)S(1)}, f32[12,3,256]{2,1,0:T(4,128)}, u32[]{:S(2)}) copy-start(f32[12,3,256]{2,1,0:T(4,128)} %refs_2_.3) | copy-start | bytes 110596
  6.9 58.4 %copy-start.16 = (s32[12,6]{0,1:T(8,128)S(1)}, s32[12,6]{0,1:T(8,128)}, u32[]{:S(2)}) copy-start(s32[12,6]{0,1:T(8,128)} %param.7) | copy-start | bytes 868
  6.9 30.8 %collective-permute-start.6 = (bf16[1584,256]{1,0:T(8,128)(2,1)}, bf16[1584,256]{1,0:T(8,128)(2,1)S(1)}, u32[]{:S(2)}, u32[]{:S(2)}) collective-permute-start(bf16[1584,256]{1,0:T(8,128)(2,1)} %shard_map.59.refs_0_), channel_id=1, source_target_pairs={{0,16},{8,24},{1,17},{9,25},{2,18},{10,26},{3,19},{11,27},{4,20},{... | collective-permute-start | bytes 2433032 | tf_op jit(solution)/shard_map/ppermute | solution.py:504
  10.5 67.5 %copy-start.5 = (bf16[864,256]{1,0:T(8,128)(2,1)}, bf16[864,256]{1,0:T(8,128)(2,1)S(1)}, u32[]{:S(2)}) copy-start(bf16[864,256]{1,0:T(8,128)(2,1)S(1)} %collective-permute-done.9.refs_2_.refs_4_.refs_11_) | copy-start | bytes 1327108
  10.6 67.5 %copy-start.6 = (bf16[864,256]{1,0:T(8,128)(2,1)}, bf16[864,256]{1,0:T(8,128)(2,1)S(1)}, u32[]{:S(2)}) copy-start(bf16[864,256]{1,0:T(8,128)(2,1)S(1)} %collective-permute-done.8.refs_1_.refs_2_.refs_9_) | copy-start | bytes 1327108
  10.6 19.5 %collective-permute-start.11 = (bf16[864,256]{1,0:T(8,128)(2,1)S(1)}, bf16[864,256]{1,0:T(8,128)(2,1)S(1)}, u32[]{:S(2)}, u32[]{:S(2)}) collective-permute-start(bf16[864,256]{1,0:T(8,128)(2,1)S(1)} %shard_map.62), channel_id=1, source_target_pairs={{4,6},{5,7},{0,1},{1,0},{12,14},{13,15},{8,9},{9,8},{20,22},{21,23... | collective-permute-start | bytes 1327112 | tf_op jit(solution)/shard_map/ppermute | solution.py:546
  11.9 18.2 %collective-permute-start.10 = (bf16[864,256]{1,0:T(8,128)(2,1)S(1)}, bf16[864,256]{1,0:T(8,128)(2,1)S(1)}, u32[]{:S(2)}, u32[]{:S(2)}) collective-permute-start(bf16[864,256]{1,0:T(8,128)(2,1)S(1)} %shard_map.62), channel_id=1, source_target_pairs={{0,4},{1,5},{4,2},{5,3},{8,12},{9,13},{12,10},{13,11},{16,20},{17,... | collective-permute-start | bytes 1327112 | tf_op jit(solution)/shard_map/ppermute | solution.py:546
  30.2 48.0 %copy-start.3 = (bf16[864,256]{1,0:T(8,128)(2,1)}, bf16[864,256]{1,0:T(8,128)(2,1)S(1)}, u32[]{:S(2)}) copy-start(bf16[864,256]{1,0:T(8,128)(2,1)S(1)} %collective-permute-done.11.refs_2_.refs_3_.refs_10_.refs_18_) | copy-start | bytes 1327108
  30.2 48.0 %copy-start.4 = (bf16[864,256]{1,0:T(8,128)(2,1)}, bf16[864,256]{1,0:T(8,128)(2,1)S(1)}, u32[]{:S(2)}) copy-start(bf16[864,256]{1,0:T(8,128)(2,1)S(1)} %collective-permute-done.10.refs_1_.refs_8_.refs_16_) | copy-start | bytes 1327108
  30.2 12.3 %collective-permute-start.13 = (bf16[864,256]{1,0:T(8,128)(2,1)S(1)}, bf16[864,256]{1,0:T(8,128)(2,1)S(1)}, u32[]{:S(2)}, u32[]{:S(2)}) collective-permute-start(bf16[864,256]{1,0:T(8,128)(2,1)S(1)} %shard_map.63), channel_id=1, source_target_pairs={{0,4},{1,5},{4,2},{5,3},{6,7},{7,6},{8,12},{9,13},{12,10},{13,11},... | collective-permute-start | bytes 1327112 | tf_op jit(solution)/shard_map/ppermute | solution.py:546
  33.6 11.7 %collective-permute-start.12 = (bf16[864,256]{1,0:T(8,128)(2,1)S(1)}, bf16[864,256]{1,0:T(8,128)(2,1)S(1)}, u32[]{:S(2)}, u32[]{:S(2)}) collective-permute-start(bf16[864,256]{1,0:T(8,128)(2,1)S(1)} %shard_map.63), channel_id=1, source_target_pairs={{4,6},{5,7},{0,1},{1,0},{2,3},{3,2},{6,5},{7,4},{12,14},{13,15},{8... | collective-permute-start | bytes 1327112 | tf_op jit(solution)/shard_map/ppermute | solution.py:546
  38.9 25.8 %collective-permute-start.7 = (bf16[1584,256]{1,0:T(8,128)(2,1)S(1)}, bf16[1584,256]{1,0:T(8,128)(2,1)S(1)}, u32[]{:S(2)}, u32[]{:S(2)}) collective-permute-start(bf16[1584,256]{1,0:T(8,128)(2,1)S(1)} %shard_map.60.mine), channel_id=1, source_target_pairs={{0,8},{8,0},{16,24},{24,16},{1,9},{9,1},{17,25},{25,17},{2,10},{10... | collective-permute-start | bytes 2433032 | tf_op jit(solution)/shard_map/ppermute | solution.py:508
  42.5 35.6 %copy-start.1 = (bf16[864,256]{1,0:T(8,128)(2,1)}, bf16[864,256]{1,0:T(8,128)(2,1)S(1)}, u32[]{:S(2)}) copy-start(bf16[864,256]{1,0:T(8,128)(2,1)S(1)} %collective-permute-done.13.refs_6_.refs_0_.refs_13_.refs_15_.refs_23_) | copy-start | bytes 1327108
  45.3 32.8 %copy-start.2 = (bf16[864,256]{1,0:T(8,128)(2,1)}, bf16[864,256]{1,0:T(8,128)(2,1)S(1)}, u32[]{:S(2)}) copy-start(bf16[864,256]{1,0:T(8,128)(2,1)S(1)} %collective-permute-done.12.refs_5_.refs_1_.refs_12_.refs_17_.refs_25_) | copy-start | bytes 1327108
  45.4 11.9 %collective-permute-start.17 = (bf16[864,256]{1,0:T(8,128)(2,1)S(1)}, bf16[864,256]{1,0:T(8,128)(2,1)S(1)}, u32[]{:S(2)}, u32[]{:S(2)}) collective-permute-start(bf16[864,256]{1,0:T(8,128)(2,1)S(1)} %shard_map.67), channel_id=1, source_target_pairs={{4,2},{5,3},{6,7},{7,6},{12,10},{13,11},{14,15},{15,14},{20,18},{2... | collective-permute-start | bytes 1327112 | tf_op jit(solution)/shard_map/ppermute | solution.py:546
  48.6 11.1 %collective-permute-start.16 = (bf16[864,256]{1,0:T(8,128)(2,1)S(1)}, bf16[864,256]{1,0:T(8,128)(2,1)S(1)}, u32[]{:S(2)}, u32[]{:S(2)}) collective-permute-start(bf16[864,256]{1,0:T(8,128)(2,1)S(1)} %shard_map.67), channel_id=1, source_target_pairs={{4,6},{5,7},{2,3},{3,2},{6,5},{7,4},{12,14},{13,15},{10,11},{11,10... | collective-permute-start | bytes 1327112 | tf_op jit(solution)/shard_map/ppermute | solution.py:546
  52.1 5.1 %collective-permute-start.14 = (bf16[272,256]{1,0:T(8,128)(2,1)S(1)}, bf16[272,256]{1,0:T(8,128)(2,1)S(1)}, u32[]{:S(2)}, u32[]{:S(2)}) collective-permute-start(bf16[272,256]{1,0:T(8,128)(2,1)S(1)} %shard_map.64.mine), channel_id=1, source_target_pairs={{0,16},{8,24},{16,0},{24,8},{1,17},{9,25},{17,1},{25,9},{2,18},{10... | collective-permute-start | bytes 417800 | tf_op jit(solution)/shard_map/ppermute | solution.py:517
  57.2 7.5 %collective-permute-start.15 = (bf16[272,256]{1,0:T(8,128)(2,1)S(1)}, bf16[272,256]{1,0:T(8,128)(2,1)S(1)}, u32[]{:S(2)}, u32[]{:S(2)}) collective-permute-start(bf16[272,256]{1,0:T(8,128)(2,1)S(1)} %shard_map.65.corner.refs_2_), channel_id=1, source_target_pairs={{0,8},{8,0},{16,24},{24,16},{1,9},{9,1},{17,25},{25,17},{2,10},{10... | collective-permute-start | bytes 417800 | tf_op jit(solution)/shard_map/ppermute | solution.py:519
  59.7 19.7 %collective-permute-start.19 = (bf16[864,256]{1,0:T(8,128)(2,1)S(1)}, bf16[864,256]{1,0:T(8,128)(2,1)S(1)}, u32[]{:S(2)}, u32[]{:S(2)}) collective-permute-start(bf16[864,256]{1,0:T(8,128)(2,1)S(1)} %shard_map.68), channel_id=1, source_target_pairs={{6,7},{7,6},{14,15},{15,14},{22,23},{23,22},{30,31},{31,30}} | collective-permute-start | bytes 1327112 | tf_op jit(solution)/shard_map/ppermute | solution.py:546
  62.2 17.3 %collective-permute-start.18 = (bf16[864,256]{1,0:T(8,128)(2,1)S(1)}, bf16[864,256]{1,0:T(8,128)(2,1)S(1)}, u32[]{:S(2)}, u32[]{:S(2)}) collective-permute-start(bf16[864,256]{1,0:T(8,128)(2,1)S(1)} %shard_map.68), channel_id=1, source_target_pairs={{2,3},{3,2},{6,5},{7,4},{10,11},{11,10},{14,13},{15,12},{18,19},{1... | collective-permute-start | bytes 1327112 | tf_op jit(solution)/shard_map/ppermute | solution.py:546
  (10 other events, 92.9 us)

commit v4 on v3

--- a/solution.py
+++ b/solution.py
@@ -12,7 +12,7 @@
 FLAG_ROWS = 16
 PIECE_ROWS = 32
 MOST_CHUNKS = 3
-BATCH = 3
+BATCH = 4
 WIDE_VMEM = 54 * 1024 * 1024
 VMEM_LIMIT = 20 * 1024 * 1024
 UPDATE_VMEM = 44 * 1024 * 1024
@@ -326,7 +326,7 @@
             copies[-1].start()
     else:
         near = given
-        outs[2][...] = extra[0][...]
+        outs[2][...] = extra[0][0:1, 0:1]
     rhs, upper, upper_one, sides, inverse = near
 
     for k, per_chunk in enumerate(sources):
@@ -360,7 +360,7 @@
     copy.wait()
 
     early = ((n - 1) * height - FLAG_ROWS) // width
-    zeroth = first = count = jnp.int32(0)
+    zeroth = first = count = vacant = jnp.int32(0)
     for i in range(rows):
         occupied = flags_s[i, 0], flags_s[FLAG_ROWS + i, 0]
         slot_zeroth, slot_first = jnp.where(occupied[0] > 0, zeroth, -1), jnp.where(occupied[1] > 0, first, -1)
@@ -368,22 +368,31 @@
         slot_of[1, i] = slot_first
         ready = (slot_zeroth < early) & (slot_first < early)
         mine = jnp.logical_not(ready) if last else ready
-        order[count] = i
-        count = count + mine.astype(jnp.int32)
+        empty = (slot_zeroth < 0) & (slot_first < 0)
+        full = mine & jnp.logical_not(empty)
+        order[jnp.where(empty, rows - 1 - vacant, count)] = i
+        count = count + full.astype(jnp.int32)
+        vacant = vacant + empty.astype(jnp.int32)
         zeroth, first = zeroth + occupied[0], first + occupied[1]
 
     def row_at(t):
         return order[jnp.minimum(t, count - 1)]
 
     def fetch(t):
-        return pltpu.make_async_copy(blocks.at[row_at(t)], work.at[t], in_sems.at[t])
+        return pltpu.make_async_copy(blocks.at[order[t]], work.at[t], in_sems.at[t])
 
     def send(t):
-        return pltpu.make_async_copy(work.at[t], out.at[row_at(t)], out_sems.at[t])
+        return pltpu.make_async_copy(work.at[t], out.at[order[t]], out_sems.at[t])
 
     @pl.loop(0, count)
     def _(t):
         fetch(t).start()
+
+    if not last:
+
+        @pl.loop(rows - vacant, rows)
+        def _(t):
+            fetch(t).start()
 
     if not last:
         forward[...] = rhs[...]
@@ -432,6 +441,19 @@
                 fresh = jnp.where(lower_first, lower[t, :, width : 2 * width], fresh)
             work[t, j] = fresh
         send(t).start()
+
+    if not last:
+
+        @pl.loop(rows - vacant, rows)
+        def _(t):
+            fetch(t).wait()
+            for j in range(cols):
+                work[t, j] = jnp.where(pattern[j, order[t]] == 1, work[t, j], zero)
+            send(t).start()
+
+        @pl.loop(rows - vacant, rows)
+        def _(t):
+            send(t).wait()
 
     @pl.loop(0, count)
     def _(t):
@@ -462,7 +484,7 @@
         scratch += [pltpu.VMEM(a.shape, a.dtype) for a in given]
         scratch += [pltpu.SemaphoreType.DMA((len(given) + 3,)), pltpu.SemaphoreType.DMA((n, 2))]
     else:
-        out_shape.append(jax.ShapeDtypeStruct(extra[0].shape, F32))
+        out_shape.append(jax.ShapeDtypeStruct((1, 1), F32))
     place = far if last else near
     arrays = (*given, *landed, *extra)
     return pl.pallas_call(

time: 88.5 us -> 87.2 us (0.985)
  the two profiles are of different devices: /device:TPU:24 before, /device:TPU:26 now
where the time goes in v4:
time: 87.2 us; the launch traced here: 86.1 us
  waiting for transfers between devices  32.8 us (38%)
  starting transfers between devices  24.7 us (28%)
  Pallas kernels  24.6 us (28%)
  local copies, waits for them, and re-layouts  2.16 us (2%)
  between operations  1.73 us (2%)
    ppermute x10, waiting for transfers between devices, travel(): return [lax.ppermute(payload, 'cols', p) if p else None for p in pairs]  28.3 us
    ppermute x10, starting transfers between devices, travel(): return [lax.ppermute(payload, 'cols', p) if p else None for p in pairs]  22.6 us
    pallas_call x2, Pallas kernels, update(): pl.pallas_call(functools.partial(update_kernel, n, height, nrows, ncols,...  19 us
    ppermute x1, waiting for transfers between devices, across_rows(): lax.ppermute(x, 'rows', [(r, r ^ 2 * reach) for r in range(nrows)])  4.52 us
    pallas_call x1, Pallas kernels, pack(): pl.pallas_call(functools.partial(pack_kernel, n, height), grid=(1,), in_s...  2.69 us
    unnamed x40, local copies, waits for them, and re-layouts  2.14 us
    pallas_call x1, Pallas kernels, pack_row(): pl.pallas_call(row_kernel, grid=(1,), in_specs=[pl.BlockSpec(memory_space...  2.09 us
  transfers between devices with their start and end apart: 14, of which 5 were waited for; matrix products, arithmetic and copies ran while one was open for 0% of the time, Pallas kernels for 14%

profile of v4, /device:TPU:26, one launch (start us, length us, event | category | flops | bytes accessed | tf_op | source)
XLA Modules:
  0.0 86.1 jit_solution(14884590146866586937)
XLA Ops:
  0.6 2.7 %shard_map.61 = (bf16[864,256]{1,0:T(8,128)(2,1)}, bf16[2,864,256]{2,1,0:T(8,128)(2,1)}, bf16[512,256]{1,0:T(8,128)(2,1)S(1)}) custom-call(s32[6,12]{1,0:T(8,128)} %bitcast.2, bf16[12,6,256,256]{3,2,1,0:T(8,128)(2,1)} %refs_1_.3), custom_call_target="tpu_custom_call" | custom-call | tf_op jit(solution)/shard_map/pallas_call | solution.py:135
  3.3 0.8 collective-permute-start.9
  4.1 0.7 collective-permute-start.8
  4.8 2.1 %shard_map.59.refs_0_ = bf16[1584,256]{1,0:T(8,128)(2,1)} custom-call(s32[6,12]{1,0:T(8,128)} %bitcast.3, bf16[12,6,256,256]{3,2,1,0:T(8,128)(2,1)} %refs_1_.3, f32[12,3,256]{2,1,0:T(4,128)} %refs_2_.3), custom_call_target="tpu_custom_call" | custom-call | tf_op jit(solution)/shard_map/pallas_call | solution.py:166
  6.9 1.4 %collective-permute-start.6 = (bf16[1584,256]{1,0:T(8,128)(2,1)}, bf16[1584,256]{1,0:T(8,128)(2,1)S(1)}, u32[]{:S(2)}, u32[]{:S(2)}) collective-permute-start(bf16[1584,256]{1,0:T(8,128)(2,1)} %shard_map.59.refs_0_), channel_id=1, source_target_pairs={{0,16},{8,24},{1,17},{9,25},{2,18},{10,26},{3,19},{11,27},{4,20},{... | collective-permute-start | bytes 2433032 | tf_op jit(solution)/shard_map/ppermute | solution.py:526
  8.4 1.3 %collective-permute-start.11 = (bf16[864,256]{1,0:T(8,128)(2,1)S(1)}, bf16[864,256]{1,0:T(8,128)(2,1)S(1)}, u32[]{:S(2)}, u32[]{:S(2)}) collective-permute-start(bf16[864,256]{1,0:T(8,128)(2,1)S(1)} %shard_map.62), channel_id=1, source_target_pairs={{4,6},{5,7},{0,1},{1,0},{12,14},{13,15},{8,9},{9,8},{20,22},{21,23... | collective-permute-start | bytes 1327112 | tf_op jit(solution)/shard_map/ppermute | solution.py:568
  9.7 0.7 collective-permute-start.10
  10.4 19.7 %collective-permute-done.11.refs_2_.refs_3_.refs_10_.refs_18_ = bf16[864,256]{1,0:T(8,128)(2,1)S(1)} collective-permute-done((bf16[864,256]{1,0:T(8,128)(2,1)S(1)}, bf16[864,256]{1,0:T(8,128)(2,1)S(1)}, u32[]{:S(2)}, u32[]{:S(2)}) %collective-permute-start.11) | collective-permute-done | bytes 442400 | tf_op jit(solution)/shard_map/ppermute | solution.py:568
  30.2 3.4 %collective-permute-start.13 = (bf16[864,256]{1,0:T(8,128)(2,1)S(1)}, bf16[864,256]{1,0:T(8,128)(2,1)S(1)}, u32[]{:S(2)}, u32[]{:S(2)}) collective-permute-start(bf16[864,256]{1,0:T(8,128)(2,1)S(1)} %shard_map.63), channel_id=1, source_target_pairs={{0,4},{1,5},{4,2},{5,3},{6,7},{7,6},{8,12},{9,13},{12,10},{13,11},... | collective-permute-start | bytes 1327112 | tf_op jit(solution)/shard_map/ppermute | solution.py:568
  33.6 4.1 %collective-permute-start.12 = (bf16[864,256]{1,0:T(8,128)(2,1)S(1)}, bf16[864,256]{1,0:T(8,128)(2,1)S(1)}, u32[]{:S(2)}, u32[]{:S(2)}) collective-permute-start(bf16[864,256]{1,0:T(8,128)(2,1)S(1)} %shard_map.63), channel_id=1, source_target_pairs={{4,6},{5,7},{0,1},{1,0},{2,3},{3,2},{6,5},{7,4},{12,14},{13,15},{8... | collective-permute-start | bytes 1327112 | tf_op jit(solution)/shard_map/ppermute | solution.py:568
  37.7 1.1 %copy-done.11 = bf16[1584,256]{1,0:T(8,128)(2,1)S(1)} copy-done((bf16[1584,256]{1,0:T(8,128)(2,1)S(1)}, bf16[1584,256]{1,0:T(8,128)(2,1)}, u32[]{:S(2)}) %copy-start.11) | copy-done | bytes 811032
  39.0 3.5 %collective-permute-done.13.refs_6_.refs_0_.refs_13_.refs_15_.refs_23_ = bf16[864,256]{1,0:T(8,128)(2,1)S(1)} collective-permute-done((bf16[864,256]{1,0:T(8,128)(2,1)S(1)}, bf16[864,256]{1,0:T(8,128)(2,1)S(1)}, u32[]{:S(2)}, u32[]{:S(2)}) %collective-permute-start.13) | collective-permute-done | bytes 442400 | tf_op jit(solution)/shard_map/ppermute | solution.py:568
  42.4 2.8 %collective-permute-done.12.refs_5_.refs_1_.refs_12_.refs_17_.refs_25_ = bf16[864,256]{1,0:T(8,128)(2,1)S(1)} collective-permute-done((bf16[864,256]{1,0:T(8,128)(2,1)S(1)}, bf16[864,256]{1,0:T(8,128)(2,1)S(1)}, u32[]{:S(2)}, u32[]{:S(2)}) %collective-permute-start.12) | collective-permute-done | bytes 442400 | tf_op jit(solution)/shard_map/ppermute | solution.py:568
  45.3 3.2 %collective-permute-start.17 = (bf16[864,256]{1,0:T(8,128)(2,1)S(1)}, bf16[864,256]{1,0:T(8,128)(2,1)S(1)}, u32[]{:S(2)}, u32[]{:S(2)}) collective-permute-start(bf16[864,256]{1,0:T(8,128)(2,1)S(1)} %shard_map.67), channel_id=1, source_target_pairs={{4,2},{5,3},{6,7},{7,6},{12,10},{13,11},{14,15},{15,14},{20,18},{2... | collective-permute-start | bytes 1327112 | tf_op jit(solution)/shard_map/ppermute | solution.py:568
  48.5 3.4 %collective-permute-start.16 = (bf16[864,256]{1,0:T(8,128)(2,1)S(1)}, bf16[864,256]{1,0:T(8,128)(2,1)S(1)}, u32[]{:S(2)}, u32[]{:S(2)}) collective-permute-start(bf16[864,256]{1,0:T(8,128)(2,1)S(1)} %shard_map.67), channel_id=1, source_target_pairs={{4,6},{5,7},{2,3},{3,2},{6,5},{7,4},{12,14},{13,15},{10,11},{11,10... | collective-permute-start | bytes 1327112 | tf_op jit(solution)/shard_map/ppermute | solution.py:568
  52.0 0.6 collective-permute-start.14
  52.6 4.5 %collective-permute-done.14.moved = bf16[272,256]{1,0:T(8,128)(2,1)S(1)} collective-permute-done((bf16[272,256]{1,0:T(8,128)(2,1)S(1)}, bf16[272,256]{1,0:T(8,128)(2,1)S(1)}, u32[]{:S(2)}, u32[]{:S(2)}) %collective-permute-start.14) | collective-permute-done | bytes 139296 | tf_op jit(solution)/shard_map/ppermute | solution.py:539
  57.3 2.3 %collective-permute-done.16.refs_1_.refs_19_.refs_24_ = bf16[864,256]{1,0:T(8,128)(2,1)S(1)} collective-permute-done((bf16[864,256]{1,0:T(8,128)(2,1)S(1)}, bf16[864,256]{1,0:T(8,128)(2,1)S(1)}, u32[]{:S(2)}, u32[]{:S(2)}) %collective-permute-start.16) | collective-permute-done | bytes 442400 | tf_op jit(solution)/shard_map/ppermute | solution.py:568
  59.6 2.5 %collective-permute-start.19 = (bf16[864,256]{1,0:T(8,128)(2,1)S(1)}, bf16[864,256]{1,0:T(8,128)(2,1)S(1)}, u32[]{:S(2)}, u32[]{:S(2)}) collective-permute-start(bf16[864,256]{1,0:T(8,128)(2,1)S(1)} %shard_map.68), channel_id=1, source_target_pairs={{6,7},{7,6},{14,15},{15,14},{22,23},{23,22},{30,31},{31,30}} | collective-permute-start | bytes 1327112 | tf_op jit(solution)/shard_map/ppermute | solution.py:568
  62.1 2.5 %collective-permute-start.18 = (bf16[864,256]{1,0:T(8,128)(2,1)S(1)}, bf16[864,256]{1,0:T(8,128)(2,1)S(1)}, u32[]{:S(2)}, u32[]{:S(2)}) collective-permute-start(bf16[864,256]{1,0:T(8,128)(2,1)S(1)} %shard_map.68), channel_id=1, source_target_pairs={{2,3},{3,2},{6,5},{7,4},{10,11},{11,10},{14,13},{15,12},{18,19},{1... | collective-permute-start | bytes 1327112 | tf_op jit(solution)/shard_map/ppermute | solution.py:568
  64.6 0.6 shard_map.66
  65.2 9.4 %shard_map.69 = (bf16[12,6,256,256]{3,2,1,0:T(8,128)(2,1)}, f32[12,3,256]{2,1,0:T(4,128)S(1)}, f32[1,1]{1,0:T(1,128)}) custom-call(s32[6,12]{1,0:T(8,128)S(1)} %bitcast.5, bf16[12,6,256,256]{3,2,1,0:T(8,128)(2,1)} %refs_1_.3, f32[12,3,256]{2,1,0:T(4,128)S(1)} %copy-done.14, bf16[512,1536]{1,0:T(8,128)(2,1)S(1)} %get-tuple-element.18.refs_3_, ...), custom_call_target="tpu_custom_call" | custom-call | flops 3221225472 | bytes 12582912 | tf_op jit(solution)/shard_map/pallas_call | solution.py:490
  75.6 0.7 copy-done.18
  76.5 9.6 %shard_map.70 = (bf16[12,6,256,256]{3,2,1,0:T(8,128)(2,1)}, f32[12,3,256]{2,1,0:T(4,128)}) custom-call(s32[6,12]{1,0:T(8,128)} %bitcast.4, bf16[12,6,256,256]{3,2,1,0:T(8,128)(2,1)} %refs_1_.3, f32[12,3,256]{2,1,0:T(4,128)} %refs_2_.3, bf16[512,1536]{1,0:T(8,128)(2,1)} %copy-done.9, bf16[256,256]{1,0:T(8,128)(2,1)} %copy-done.13, ...), custom_call_target="tpu_custom_call", output_to_operand_aliasing={{0}: (31, {})} | custom-call | flops 3221225472 | bytes 12582912 | tf_op jit(solution)/shard_map/pallas_call | solution.py:490
  (58 shorter events, 0.8 us)
Async XLA Ops:
  3.3 48.6 %copy-start.10 = (bf16[864,256]{1,0:T(8,128)(2,1)S(1)}, bf16[864,256]{1,0:T(8,128)(2,1)}, u32[]{:S(2)}) copy-start(bf16[864,256]{1,0:T(8,128)(2,1)} %get-tuple-element.16.refs_0_.refs_7_) | copy-start | bytes 1327108
  3.3 61.3 %copy-start.12 = (bf16[2,256,256]{2,1,0:T(8,128)(2,1)S(1)}, bf16[2,256,256]{2,1,0:T(8,128)(2,1)}, u32[]{:S(2)}) copy-start(bf16[2,256,256]{2,1,0:T(8,128)(2,1)} %refs_6_.3) | copy-start | bytes 786436
  3.3 5.0 %collective-permute-start.9 = (bf16[864,256]{1,0:T(8,128)(2,1)}, bf16[864,256]{1,0:T(8,128)(2,1)S(1)}, u32[]{:S(2)}, u32[]{:S(2)}) collective-permute-start(bf16[864,256]{1,0:T(8,128)(2,1)} %get-tuple-element.16.refs_0_.refs_7_), channel_id=1, source_target_pairs={{0,1},{1,0},{8,9},{9,8},{16,17},{17,16},{24,25},{25,24}} | collective-permute-start | bytes 1327112 | tf_op jit(solution)/shard_map/ppermute | solution.py:568
  4.1 4.2 %collective-permute-start.8 = (bf16[864,256]{1,0:T(8,128)(2,1)}, bf16[864,256]{1,0:T(8,128)(2,1)S(1)}, u32[]{:S(2)}, u32[]{:S(2)}) collective-permute-start(bf16[864,256]{1,0:T(8,128)(2,1)} %get-tuple-element.16.refs_0_.refs_7_), channel_id=1, source_target_pairs={{0,4},{1,5},{8,12},{9,13},{16,20},{17,21},{24,28},{25,29}} | collective-permute-start | bytes 1327112 | tf_op jit(solution)/shard_map/ppermute | solution.py:568
  6.9 58.3 %copy-start.14 = (f32[12,3,256]{2,1,0:T(4,128)S(1)}, f32[12,3,256]{2,1,0:T(4,128)}, u32[]{:S(2)}) copy-start(f32[12,3,256]{2,1,0:T(4,128)} %refs_2_.3) | copy-start | bytes 110596
  6.9 58.3 %copy-start.16 = (s32[12,6]{0,1:T(8,128)S(1)}, s32[12,6]{0,1:T(8,128)}, u32[]{:S(2)}) copy-start(s32[12,6]{0,1:T(8,128)} %param.7) | copy-start | bytes 868
  6.9 30.7 %collective-permute-start.6 = (bf16[1584,256]{1,0:T(8,128)(2,1)}, bf16[1584,256]{1,0:T(8,128)(2,1)S(1)}, u32[]{:S(2)}, u32[]{:S(2)}) collective-permute-start(bf16[1584,256]{1,0:T(8,128)(2,1)} %shard_map.59.refs_0_), channel_id=1, source_target_pairs={{0,16},{8,24},{1,17},{9,25},{2,18},{10,26},{3,19},{11,27},{4,20},{... | collective-permute-start | bytes 2433032 | tf_op jit(solution)/shard_map/ppermute | solution.py:526
  8.4 66.3 %copy-start.5 = (bf16[864,256]{1,0:T(8,128)(2,1)}, bf16[864,256]{1,0:T(8,128)(2,1)S(1)}, u32[]{:S(2)}) copy-start(bf16[864,256]{1,0:T(8,128)(2,1)S(1)} %collective-permute-done.9.refs_2_.refs_4_.refs_11_) | copy-start | bytes 1327108
  8.4 66.3 %copy-start.6 = (bf16[864,256]{1,0:T(8,128)(2,1)}, bf16[864,256]{1,0:T(8,128)(2,1)S(1)}, u32[]{:S(2)}) copy-start(bf16[864,256]{1,0:T(8,128)(2,1)S(1)} %collective-permute-done.8.refs_1_.refs_2_.refs_9_) | copy-start | bytes 1327108
  8.4 21.7 %collective-permute-start.11 = (bf16[864,256]{1,0:T(8,128)(2,1)S(1)}, bf16[864,256]{1,0:T(8,128)(2,1)S(1)}, u32[]{:S(2)}, u32[]{:S(2)}) collective-permute-start(bf16[864,256]{1,0:T(8,128)(2,1)S(1)} %shard_map.62), channel_id=1, source_target_pairs={{4,6},{5,7},{0,1},{1,0},{12,14},{13,15},{8,9},{9,8},{20,22},{21,23... | collective-permute-start | bytes 1327112 | tf_op jit(solution)/shard_map/ppermute | solution.py:568
  9.7 20.4 %collective-permute-start.10 = (bf16[864,256]{1,0:T(8,128)(2,1)S(1)}, bf16[864,256]{1,0:T(8,128)(2,1)S(1)}, u32[]{:S(2)}, u32[]{:S(2)}) collective-permute-start(bf16[864,256]{1,0:T(8,128)(2,1)S(1)} %shard_map.62), channel_id=1, source_target_pairs={{0,4},{1,5},{4,2},{5,3},{8,12},{9,13},{12,10},{13,11},{16,20},{17,... | collective-permute-start | bytes 1327112 | tf_op jit(solution)/shard_map/ppermute | solution.py:568
  30.1 44.6 %copy-start.3 = (bf16[864,256]{1,0:T(8,128)(2,1)}, bf16[864,256]{1,0:T(8,128)(2,1)S(1)}, u32[]{:S(2)}) copy-start(bf16[864,256]{1,0:T(8,128)(2,1)S(1)} %collective-permute-done.11.refs_2_.refs_3_.refs_10_.refs_18_) | copy-start | bytes 1327108
  30.1 44.6 %copy-start.4 = (bf16[864,256]{1,0:T(8,128)(2,1)}, bf16[864,256]{1,0:T(8,128)(2,1)S(1)}, u32[]{:S(2)}) copy-start(bf16[864,256]{1,0:T(8,128)(2,1)S(1)} %collective-permute-done.10.refs_1_.refs_8_.refs_16_) | copy-start | bytes 1327108
  30.2 12.3 %collective-permute-start.13 = (bf16[864,256]{1,0:T(8,128)(2,1)S(1)}, bf16[864,256]{1,0:T(8,128)(2,1)S(1)}, u32[]{:S(2)}, u32[]{:S(2)}) collective-permute-start(bf16[864,256]{1,0:T(8,128)(2,1)S(1)} %shard_map.63), channel_id=1, source_target_pairs={{0,4},{1,5},{4,2},{5,3},{6,7},{7,6},{8,12},{9,13},{12,10},{13,11},... | collective-permute-start | bytes 1327112 | tf_op jit(solution)/shard_map/ppermute | solution.py:568
  33.6 11.7 %collective-permute-start.12 = (bf16[864,256]{1,0:T(8,128)(2,1)S(1)}, bf16[864,256]{1,0:T(8,128)(2,1)S(1)}, u32[]{:S(2)}, u32[]{:S(2)}) collective-permute-start(bf16[864,256]{1,0:T(8,128)(2,1)S(1)} %shard_map.63), channel_id=1, source_target_pairs={{4,6},{5,7},{0,1},{1,0},{2,3},{3,2},{6,5},{7,4},{12,14},{13,15},{8... | collective-permute-start | bytes 1327112 | tf_op jit(solution)/shard_map/ppermute | solution.py:568
  38.9 25.7 %collective-permute-start.7 = (bf16[1584,256]{1,0:T(8,128)(2,1)S(1)}, bf16[1584,256]{1,0:T(8,128)(2,1)S(1)}, u32[]{:S(2)}, u32[]{:S(2)}) collective-permute-start(bf16[1584,256]{1,0:T(8,128)(2,1)S(1)} %shard_map.60.mine), channel_id=1, source_target_pairs={{0,8},{8,0},{16,24},{24,16},{1,9},{9,1},{17,25},{25,17},{2,10},{10... | collective-permute-start | bytes 2433032 | tf_op jit(solution)/shard_map/ppermute | solution.py:530
  42.4 32.3 %copy-start.1 = (bf16[864,256]{1,0:T(8,128)(2,1)}, bf16[864,256]{1,0:T(8,128)(2,1)S(1)}, u32[]{:S(2)}) copy-start(bf16[864,256]{1,0:T(8,128)(2,1)S(1)} %collective-permute-done.13.refs_6_.refs_0_.refs_13_.refs_15_.refs_23_) | copy-start | bytes 1327108
  45.3 29.4 %copy-start.2 = (bf16[864,256]{1,0:T(8,128)(2,1)}, bf16[864,256]{1,0:T(8,128)(2,1)S(1)}, u32[]{:S(2)}) copy-start(bf16[864,256]{1,0:T(8,128)(2,1)S(1)} %collective-permute-done.12.refs_5_.refs_1_.refs_12_.refs_17_.refs_25_) | copy-start | bytes 1327108
  45.3 11.9 %collective-permute-start.17 = (bf16[864,256]{1,0:T(8,128)(2,1)S(1)}, bf16[864,256]{1,0:T(8,128)(2,1)S(1)}, u32[]{:S(2)}, u32[]{:S(2)}) collective-permute-start(bf16[864,256]{1,0:T(8,128)(2,1)S(1)} %shard_map.67), channel_id=1, source_target_pairs={{4,2},{5,3},{6,7},{7,6},{12,10},{13,11},{14,15},{15,14},{20,18},{2... | collective-permute-start | bytes 1327112 | tf_op jit(solution)/shard_map/ppermute | solution.py:568
  48.5 11.1 %collective-permute-start.16 = (bf16[864,256]{1,0:T(8,128)(2,1)S(1)}, bf16[864,256]{1,0:T(8,128)(2,1)S(1)}, u32[]{:S(2)}, u32[]{:S(2)}) collective-permute-start(bf16[864,256]{1,0:T(8,128)(2,1)S(1)} %shard_map.67), channel_id=1, source_target_pairs={{4,6},{5,7},{2,3},{3,2},{6,5},{7,4},{12,14},{13,15},{10,11},{11,10... | collective-permute-start | bytes 1327112 | tf_op jit(solution)/shard_map/ppermute | solution.py:568
  52.0 5.1 %collective-permute-start.14 = (bf16[272,256]{1,0:T(8,128)(2,1)S(1)}, bf16[272,256]{1,0:T(8,128)(2,1)S(1)}, u32[]{:S(2)}, u32[]{:S(2)}) collective-permute-start(bf16[272,256]{1,0:T(8,128)(2,1)S(1)} %shard_map.64.mine), channel_id=1, source_target_pairs={{0,16},{8,24},{16,0},{24,8},{1,17},{9,25},{17,1},{25,9},{2,18},{10... | collective-permute-start | bytes 417800 | tf_op jit(solution)/shard_map/ppermute | solution.py:539
  57.2 7.4 %collective-permute-start.15 = (bf16[272,256]{1,0:T(8,128)(2,1)S(1)}, bf16[272,256]{1,0:T(8,128)(2,1)S(1)}, u32[]{:S(2)}, u32[]{:S(2)}) collective-permute-start(bf16[272,256]{1,0:T(8,128)(2,1)S(1)} %shard_map.65.corner.refs_2_), channel_id=1, source_target_pairs={{0,8},{8,0},{16,24},{24,16},{1,9},{9,1},{17,25},{25,17},{2,10},{10... | collective-permute-start | bytes 417800 | tf_op jit(solution)/shard_map/ppermute | solution.py:541
  59.6 15.9 %collective-permute-start.19 = (bf16[864,256]{1,0:T(8,128)(2,1)S(1)}, bf16[864,256]{1,0:T(8,128)(2,1)S(1)}, u32[]{:S(2)}, u32[]{:S(2)}) collective-permute-start(bf16[864,256]{1,0:T(8,128)(2,1)S(1)} %shard_map.68), channel_id=1, source_target_pairs={{6,7},{7,6},{14,15},{15,14},{22,23},{23,22},{30,31},{31,30}} | collective-permute-start | bytes 1327112 | tf_op jit(solution)/shard_map/ppermute | solution.py:568
  62.1 13.4 %collective-permute-start.18 = (bf16[864,256]{1,0:T(8,128)(2,1)S(1)}, bf16[864,256]{1,0:T(8,128)(2,1)S(1)}, u32[]{:S(2)}, u32[]{:S(2)}) collective-permute-start(bf16[864,256]{1,0:T(8,128)(2,1)S(1)} %shard_map.68), channel_id=1, source_target_pairs={{2,3},{3,2},{6,5},{7,4},{10,11},{11,10},{14,13},{15,12},{18,19},{1... | collective-permute-start | bytes 1327112 | tf_op jit(solution)/shard_map/ppermute | solution.py:568
  (10 other events, 72.0 us)
